TPU v7x, 512 devices: a whole 4x8x8 slice. The times are simulated.
512 devices in a mesh: group: 4 (over z_hi), seq: 16 (over y, core), dp: 8 (over x, z_lo).
Axes of the slice: x: 4, y: 8, z: 8 (z_hi: 4, z_lo: 2; z = z_hi * 2 + z_lo), core: 2. Of those that a mesh axis runs over, the one named last changes fastest.
Arguments:
- noise_gen: bfloat16 [16, 1024, 64], P('dp', 'seq'), may hold values from -6 to 6
- noise_score: bfloat16 [16, 1024, 64], P('dp', 'seq'), may hold values from -6 to 6
- prev_latents: float32 [16, 1024, 64], P('dp', 'seq'), may hold values from -42 to 42
- t_idx: int32 [16], P('dp'), may hold values from 0 to 999
- w_in: bfloat16 [4, 64, 3072], P('group'), may hold values from -4 to 4, as said below
- w_qkv: bfloat16 [4, 3072, 3, 2048], P('group', None, None, 'seq'), may hold values from -4 to 4, as said below
- w_out: bfloat16 [4, 2048, 64], P('group', 'seq'), may hold values from -4 to 4, as said below
- w_final: bfloat16 [4, 3072, 64], P('group'), may hold values from -4 to 4, as said below
- mod_scale: float32 [4, 3072], P('group'), may hold values from -0.5 to 0.5
- mod_shift: float32 [4, 3072], P('group'), may hold values from -3 to 3
- saved_features: bfloat16 [16, 1024, 3072], P('dp', 'seq'), may hold values from -6 to 6
Outputs:
- predictions: float32 [4, 16, 1024, 64], P('group', 'dp', 'seq')
- dmd_grad: float32 [16, 1024, 64], P('dp', 'seq')
- gen_final_grad: float32 [3072, 64], replicated
Inputs may be any that keep to these rules, and one draw needn't show every extreme that they name: `w_in`: groups 1 and 2 hold equal weights. `w_qkv`: groups 1 and 2 hold equal weights. `w_out`: groups 1 and 2 hold equal weights. `w_final`: groups 1 and 2 hold equal weights.
All inputs are finite; a program needn't handle non-finite values. Where the computation divides by a largest or mean magnitude, that divisor is 1e-20 or more.
Results may differ from a plain program's by a relative error of at most 0.017.
Values may be sent and summed in bfloat16 or wider, within the bound.
No kernel may reach another device: no remote copies, remote signals or barrier semaphores. Data moves between devices by JAX's collectives and lax.ppermute only.
A program may use at most 128 MiB of HBM per device.

v0:
```python
import math

import jax
import jax.numpy as jnp
from jax import lax
from jax.sharding import PartitionSpec as P

NTOK = 1024
NOISE_LEVEL_COUNT = 1000


def embed(latent, noise_level, w_in_here, scale, shift):
    projected = jnp.einsum("inp,pd->ind", latent, w_in_here, preferred_element_type=jnp.float32)
    normed = projected * lax.rsqrt(jnp.mean(projected * projected, axis=-1, keepdims=True) + 1e-06)
    return (normed * (1.0 + noise_level[:, None, None] * scale) + shift).astype(jnp.bfloat16)


def per_device(
    noise_gen,
    noise_score,
    prev_latents,
    t_idx,
    w_in,
    w_qkv,
    w_out,
    w_final,
    mod_scale,
    mod_shift,
    saved_features,
):
    model_index = lax.axis_index("group")
    local_image_batch, rows_image, channels = noise_gen.shape
    width = w_in.shape[2]
    head_size = w_out.shape[1]
    level = (t_idx.astype(jnp.float32) + 0.5) / NOISE_LEVEL_COUNT
    noisy = (1.0 - level)[:, None, None] * prev_latents + level[:, None, None] * noise_score.astype(
        jnp.float32
    )
    is_generator = model_index == 0
    model_input = jnp.where(is_generator, noise_gen.astype(jnp.float32), noisy)
    noise_level = jnp.where(is_generator, jnp.ones_like(level), level)
    latent = model_input.astype(jnp.bfloat16)
    w_in_here = w_in[0]
    head_weight = w_qkv[0].reshape(width, 3 * head_size)
    scale = mod_scale[0]
    shift = mod_shift[0]
    features = embed(latent, noise_level, w_in_here, scale, shift)
    triple = jnp.einsum(
        "ind,de->ine",
        lax.all_gather(features, "seq", axis=1, tiled=True),
        head_weight,
        preferred_element_type=jnp.float32,
    ).astype(jnp.bfloat16)
    queries = triple[:, :, :head_size]
    keys = triple[:, :, head_size : 2 * head_size]
    value_rows = triple[:, :, 2 * head_size :]
    scores = jnp.einsum(
        "iqe,ike->iqk", queries, keys, preferred_element_type=jnp.float32
    ) / math.sqrt(head_size)
    probs = jax.nn.softmax(scores, axis=-1).astype(jnp.bfloat16)
    attention_result = jnp.einsum(
        "iqk,ike->iqe", probs, value_rows, preferred_element_type=jnp.float32
    ).astype(jnp.bfloat16)
    token_leading_layout = attention_result.transpose(1, 0, 2)
    output_layout = w_out[0]
    summed = (
        lax.psum_scatter(
            jnp.einsum(
                "sca,af->scf",
                token_leading_layout,
                output_layout,
                preferred_element_type=jnp.float32,
            ).astype(jnp.bfloat16),
            "seq",
            scatter_dimension=0,
            tiled=True,
        )
        .astype(jnp.float32)
        .transpose(1, 0, 2)
    )
    velocity = (
        jnp.einsum("ind,dp->inp", features, w_final[0], preferred_element_type=jnp.float32) + summed
    )
    prediction = model_input - noise_level[:, None, None] * velocity
    real_weight = jnp.where(model_index == 1, 2.5, jnp.where(model_index == 2, -1.5, 0.0))
    fake_weight = jnp.where(model_index == 3, 1.0, 0.0)
    real, fake = lax.psum((real_weight * prediction, fake_weight * prediction), "group")
    deviation = jnp.sum(jnp.abs(prev_latents - real), axis=(1, 2))
    total_dev = lax.psum(deviation, "seq")
    spread = total_dev / (NTOK * channels) + 1e-05
    dmd_grad = (fake - real) / spread[:, None, None]
    down = (-dmd_grad).astype(jnp.bfloat16)
    normalizer = 1.0 / math.sqrt(local_image_batch * lax.axis_size("dp") * NTOK)
    partial_grad = jnp.einsum(
        "ind,inp->dp", saved_features, down, preferred_element_type=jnp.float32
    )
    total_grad = lax.psum(partial_grad, ("seq", "dp"))
    return (prediction[None], dmd_grad, total_grad * normalizer)


def solution(mesh):
    placed = (
        P("dp", "seq", None),
        P("dp", "seq", None),
        P("dp", "seq", None),
        P("dp"),
        P("group", None, None),
        P("group", None, None, "seq"),
        P("group", "seq", None),
        P("group", None, None),
        P("group", None),
        P("group", None),
        P("dp", "seq", None),
    )
    return jax.shard_map(
        per_device,
        mesh=mesh,
        in_specs=placed,
        out_specs=(P("group", "dp", "seq", None), P("dp", "seq", None), P()),
        check_vma=False,
    )
```

profile of v0, /device:TPU:1, one launch (start us, length us, event | category | flops | bytes accessed | tf_op | source)
XLA Modules:
  0.0 1320.2 jit_solution(8520445756125408888)
XLA Ops:
  7.2 0.0 copy-start
  7.2 0.0 all-gather.2.cloned.1.call-start
  7.2 0.7 broadcast_select_fusion
  8.0 0.0 copy-start.2
  8.0 1.7 multiply_reduce_fusion.1
  9.7 0.8 multiply_add_fusion
  10.5 1.9 add_convert_fusion
  12.3 0.0 all-gather.2.cloned.1.call-update
  12.3 0.0 reduce-scatter.2.cloned.1.call-start
  12.4 0.0 copy-done.2
  12.4 2.5 copy.15
  14.9 81.5 %all-gather.2.cloned.1.call-done = bf16[2,1024,3072]{2,1,0:T(8,128)(2,1)} async-done(((bf16[2,64,3072]{2,1,0:T(8,128)(2,1)}), bf16[2,1024,3072]{2,1,0:T(8,128)(2,1)}) %all-gather.2.cloned.1.call-update) | async-done | bytes 12582928 | tf_op jit(solution)/shard_map/all_gather | solution.py:50
  96.4 11.3 convolution_convert_fusion
  107.7 0.0 copy-start.8
  107.7 7.1 fusion.31
  114.8 0.0 copy-done.8
  114.8 0.0 copy-start.1
  114.8 0.0 copy-start.3
  114.8 0.0 copy-start.4
  114.8 0.0 copy-start.6
  114.9 0.0 copy-start.7
  114.9 6.2 convolution_convert_fusion.1
  121.0 0.0 reduce-scatter.2.cloned.1.call-update
  121.0 0.0 all-reduce.6.cloned.1.call-start
  121.1 55.8 %reduce-scatter.2.cloned.1.call-done = bf16[64,2,64]{2,0,1:T(8,128)(2,1)} async-done(((bf16[1024,2,64]{2,0,1:T(8,128)(2,1)}), bf16[64,2,64]{2,0,1:T(8,128)(2,1)}) %reduce-scatter.2.cloned.1.call-update) | async-done | bytes 16400 | tf_op jit(solution)/shard_map/reduce_scatter | solution.py:67
  176.9 0.0 copy-done.1
  176.9 0.0 copy-done.3
  176.9 0.0 copy-done.4
  176.9 0.0 copy-done.6
  176.9 0.0 copy-done.7
  177.0 1.8 broadcast_multiply_fusion.1
  178.7 0.0 all-reduce.6.cloned.1.call-update
  178.8 0.0 all-reduce.4.cloned.1.call-start
  178.8 56.7 %all-reduce.6.cloned.1.call-done = (f32[2,64,64]{2,1,0:T(8,128)}, f32[2,64,64]{2,1,0:T(8,128)}) async-done(((f32[2,64,64]{2,1,0:T(8,128)}, f32[2,64,64]{2,1,0:T(8,128)}), (f32[2,64,64]{2,1,0:T(8,128)}, f32[2,64,64]{2,1,0:T(8,128)})) %all-reduce.6.cloned.1.call-update) | async-done | bytes 65552 | tf_op jit(solution)/shard_map/psum | solution.py:87
  235.5 0.9 abs_reduce_fusion
  236.5 25.7 %psum.30 = f32[2]{0:T(128)S(1)} all-reduce(f32[2]{0:T(128)S(1)} %abs_reduce_fusion), channel_id=1, replica_groups=mesh['group'=4,'seq'=16,'dp'=8] {'seq'}, use_global_device_ids=true, to_apply=%region_7.8 | all-reduce | flops 2 | bytes 16 | tf_op jit(solution)/shard_map/psum | solution.py:89
  262.2 0.9 subtract_divide_fusion
  263.1 0.0 copy-done
  263.1 0.0 copy-start.5
  263.1 1.2 convolution_bitcast_fusion
  264.3 0.0 all-reduce.4.cloned.1.call-update
  264.3 1047.2 %all-reduce.4.cloned.1.call-done = f32[3072,64]{0,1:T(8,128)} async-done(((f32[3072,64]{0,1:T(8,128)}), f32[3072,64]{0,1:T(8,128)}) %all-reduce.4.cloned.1.call-update) | async-done | bytes 786448 | tf_op jit(solution)/shard_map/psum | solution.py:97
  1311.5 2.1 broadcast_multiply_fusion
  1313.6 0.0 copy-done.5
  (2 shorter events, 0.0 us)
Async XLA Ops:
  7.2 255.9 %copy-start = (bf16[2,64,3072]{2,1,0:T(8,128)(2,1)S(1)}, bf16[2,64,3072]{2,1,0:T(8,128)(2,1)}, u32[]{:S(2)}) copy-start(bf16[2,64,3072]{2,1,0:T(8,128)(2,1)} %param.21) | copy-start | bytes 2359300
  7.2 89.2 %all-gather.2.cloned.1.call-start = ((), (), s32[]{:S(2)}) async-start(), calls=%async_computation.1 | async-start | bytes 13369344 | tf_op jit(solution)/shard_map/all_gather | solution.py:50
  8.0 4.4 copy-start.2
  12.3 164.6 %reduce-scatter.2.cloned.1.call-start = ((), (), s32[]{:S(2)}) async-start(), calls=%async_computation.2 | async-start | bytes 557056 | tf_op jit(solution)/shard_map/reduce_scatter | solution.py:67
  107.7 7.1 copy-start.8
  114.8 62.1 %copy-start.1 = (bf16[2,64,3072]{2,1,0:T(8,128)(2,1)S(1)}, bf16[2,64,3072]{2,1,0:T(8,128)(2,1)}, u32[]{:S(2)}) copy-start(bf16[2,64,3072]{2,1,0:T(8,128)(2,1)} %add_convert_fusion) | copy-start | bytes 2359300
  114.8 62.1 %copy-start.3 = (f32[2,64,64]{2,1,0:T(8,128)S(1)}, f32[2,64,64]{2,1,0:T(8,128)}, u32[]{:S(2)}) copy-start(f32[2,64,64]{2,1,0:T(8,128)} %param.13) | copy-start | bytes 98308
  114.8 62.1 %copy-start.4 = (bf16[1,3072,64]{1,2,0:T(8,128)(2,1)S(1)}, bf16[1,3072,64]{1,2,0:T(8,128)(2,1)}, u32[]{:S(2)}) copy-start(bf16[1,3072,64]{1,2,0:T(8,128)(2,1)} %param.18) | copy-start | bytes 1179652
  114.8 62.1 %copy-start.6 = (bf16[2,64,64]{2,1,0:T(8,128)(2,1)S(1)}, bf16[2,64,64]{2,1,0:T(8,128)(2,1)}, u32[]{:S(2)}) copy-start(bf16[2,64,64]{2,1,0:T(8,128)(2,1)} %param.12) | copy-start | bytes 49156
  114.9 62.1 %copy-start.7 = (bf16[2,64,64]{2,1,0:T(8,128)(2,1)S(1)}, bf16[2,64,64]{2,1,0:T(8,128)(2,1)}, u32[]{:S(2)}) copy-start(bf16[2,64,64]{2,1,0:T(8,128)(2,1)} %param.11) | copy-start | bytes 49156
  121.0 114.5 %all-reduce.6.cloned.1.call-start = ((), (), s32[]{:S(2)}) async-start(), calls=%async_computation.4 | async-start | bytes 262144 | tf_op jit(solution)/shard_map/psum | solution.py:87
  178.8 1132.8 %all-reduce.4.cloned.1.call-start = ((), (), s32[]{:S(2)}) async-start(), calls=%async_computation.3 | async-start | bytes 1572864 | tf_op jit(solution)/shard_map/psum | solution.py:97
  263.1 1050.5 %copy-start.5 = (f32[2,64,64]{2,1,0:T(8,128)}, f32[2,64,64]{2,1,0:T(8,128)S(1)}, u32[]{:S(2)}) copy-start(f32[2,64,64]{2,1,0:T(8,128)S(1)} %subtract_divide_fusion) | copy-start | bytes 98308
Sparse Core Ops, SparseCore 0:
  12.5 83.8 all-gather.1
  121.2 55.7 reduce-scatter.1
  180.7 54.7 all-reduce.5
  264.4 1047.0 all-reduce.3
where the time goes:
time: 1320 us
  waiting for transfers between devices  1240 us (94%)
  matrix products  29.3 us (2%)
  blocking collectives  25.7 us (2%)
  between operations  13.9 us (1%)
    psum x1, waiting for transfers between devices, per_device(): total_grad = lax.psum(partial_grad, ('seq', 'dp'))  1050 us
    all_gather x1, waiting for transfers between devices, per_device(): lax.all_gather(features, 'seq', axis=1, tiled=True)  81.5 us
    psum x1, waiting for transfers between devices, per_device(): lax.psum((real_weight * prediction, fake_weight * prediction), 'group')  56.7 us
    reduce_scatter x1, waiting for transfers between devices, per_device(): lax.psum_scatter(jnp.einsum('sca,af->scf', token_leading_layout, output_l...  55.8 us
  transfers between devices with their start and end apart: 4, of which 4 were waited for; matrix products, arithmetic and copies ran while one was open for 0% of the time, Pallas kernels for 0%

commit v1 on v0

v1 whole, which is shorter than its diff:
```python
import math

import jax
import jax.numpy as jnp
from jax import lax
from jax.experimental import pallas as pl
from jax.experimental.pallas import tpu as pltpu
from jax.sharding import PartitionSpec as P

NTOK = 1024
NOISE_LEVEL_COUNT = 1000
BF16 = jnp.bfloat16
F32 = jnp.float32
ROWS = 208


def dot(a, b, lhs=1, rhs=0):
    return lax.dot_general(a, b, (((lhs,), (rhs,)), ((), ())), preferred_element_type=F32)


def left_half(shape):
    return lax.broadcasted_iota(jnp.int32, shape, 1) < 64


def levels(group_ref, t_ref):
    gen = jnp.where(group_ref[0] == 0, 1.0, 0.0).astype(F32)
    level = [(t_ref[i].astype(F32) + 0.5) * (1.0 / NOISE_LEVEL_COUNT) for i in range(2)]
    return gen, level, [gen + (1.0 - gen) * value for value in level]


def noisy_latent(level, prev, noise):
    return (1.0 - level) * prev + level * noise.astype(F32)


def fold_kernel(
    group_ref, t_ref, gen_ref, noise_ref, prev_ref, w_in_ref, w_qkv_ref, w_out_ref, w_final_ref,
    scale_ref, shift_ref, sent_ref, local_ref, left_ref,
):
    width = w_in_ref.shape[2]
    gen, level, used = levels(group_ref, t_ref)
    latents = []
    for i in range(2):
        noisy = noisy_latent(level[i], prev_ref[i], noise_ref[i])
        latents.append(gen * gen_ref[i].astype(F32) + (1.0 - gen) * noisy)
    latent = jnp.concatenate(latents, axis=0).astype(BF16)
    step = 512
    squares = jnp.zeros((128, step), F32)
    for at in range(0, width, step):
        part = w_in_ref[0, :, at : at + step]
        projected = dot(latent, part)
        squares = squares + projected * projected
        scale = scale_ref[:, at : at + step]
        shift = shift_ref[:, at : at + step]
        high = shift.astype(BF16).astype(F32)
        row = lax.broadcasted_iota(jnp.int32, (16, step), 0)
        left_ref[0:64, at : at + step] = part
        left_ref[64:128, at : at + step] = (part.astype(F32) * scale).astype(BF16)
        left_ref[128:144, at : at + step] = jnp.where(
            row == 0, high, jnp.where(row == 1, shift - high, 0.0)
        ).astype(BF16)
    mean = jnp.sum(squares, axis=1, keepdims=True) * (1.0 / width)
    scaled = (latent.astype(F32) * lax.rsqrt(mean + 1e-06)).astype(BF16)
    sent_ref[144:208, :] = jnp.concatenate([scaled[0:64], scaled[64:128]], axis=1)

    folded = [dot(left_ref[...], w_qkv_ref[c]) for c in range(3)]
    final = dot(left_ref[...], w_final_ref[...], 1, 1)
    const = [part[128:129] + part[129:130] for part in folded]
    final_const = final[128:129] + final[129:130]
    factor = math.log2(math.e) / math.sqrt(128.0)
    w_out = w_out_ref[...]
    blocks, consts, locals_ = [], [], []
    value_const = dot(jnp.broadcast_to(const[2], (16, 128)).astype(BF16), w_out, 1, 1)
    for i in range(2):
        q, k, v = [(part[0:64] + used[i] * part[64:128]) for part in folded]
        kb = k.astype(BF16)
        scores = dot(q.astype(BF16), kb, 1, 1) * factor
        out = dot(v.astype(BF16), w_out, 1, 1)
        key_const = dot(jnp.broadcast_to(const[0], (16, 128)).astype(BF16), kb, 1, 1) * factor
        local = final[0:64] + used[i] * final[64:128]
        zero = jnp.zeros_like(local)
        if i == 0:
            blocks.append(jnp.concatenate([scores, out], axis=1))
            consts.append(jnp.concatenate([key_const, value_const], axis=1))
            locals_.append(jnp.concatenate([zero, local], axis=1))
        else:
            blocks.append(jnp.concatenate([out, scores], axis=1))
            consts.append(jnp.concatenate([value_const, key_const], axis=1))
            locals_.append(jnp.concatenate([local, zero], axis=1))
    sent_ref[0:64, :] = blocks[0].astype(BF16)
    sent_ref[64:128, :] = blocks[1].astype(BF16)
    row = lax.broadcasted_iota(jnp.int32, (16, 128), 0)
    sent_ref[128:144, :] = jnp.where(row == 0, consts[0], consts[1]).astype(BF16)
    local_ref[0:64, :] = locals_[0]
    local_ref[64:128, :] = locals_[1]
    both = jnp.concatenate([final_const, final_const], axis=1)
    local_ref[128:136, :] = jnp.broadcast_to(both, (8, 128))


def attend_kernel(
    group_ref, t_ref, gen_ref, noise_ref, prev_ref, all_ref, own_ref, local_ref,
    moved_ref, prediction_ref, keys_ref, query_ref, mixed_ref,
):
    heads = all_ref.shape[0]
    gen, level, used = levels(group_ref, t_ref)
    for s in range(heads):
        keys_ref[64 * s : 64 * s + 64, 0:128] = all_ref[s, 144:208, :]
    keys_ref[:, 128:256] = jnp.ones((64 * heads, 128), BF16)
    left = left_half((64, 128))
    own = own_ref[144:208, :].astype(F32)
    stacked = jnp.concatenate([jnp.where(left, own, 0.0), jnp.where(left, 0.0, own)], axis=0)
    stacked = stacked.astype(BF16)
    const_sum = jnp.zeros((16, 128), F32)
    for h in range(heads):
        block = all_ref[h, 0:128, :]
        const = all_ref[h, 128:144, :].astype(F32)
        const_sum = const_sum + const
        query = dot(stacked, block)
        rows = slice(64 * h, 64 * h + 64)
        query_ref[0, rows, :] = jnp.where(left, query[0:64] + const[0:1], 0.0).astype(BF16)
        query_ref[1, rows, :] = jnp.where(left, 0.0, query[64:128] + const[1:2]).astype(BF16)
    step = 256
    wide_left = left_half((step, 128))
    for i in range(2):
        for at in range(0, 64 * heads, step):
            rows = slice(at, at + step)
            scores = dot(query_ref[i, rows, :], keys_ref[:, 0:128], 1, 1)
            top = jnp.max(scores, axis=1, keepdims=True)
            weights = jnp.exp2(scores - top).astype(BF16)
            mixed = dot(weights, keys_ref[...])
            mixed = mixed[:, 0:128] / mixed[:, 128:256]
            keep = wide_left if i == 0 else jnp.logical_not(wide_left)
            mixed_ref[i, rows, :] = jnp.where(keep, mixed, 0.0).astype(BF16)
    total = dot(stacked, local_ref[0:128, :].astype(BF16))
    for h in range(heads):
        rows = slice(64 * h, 64 * h + 64)
        pair = jnp.concatenate([mixed_ref[0, rows, :], mixed_ref[1, rows, :]], axis=0)
        total = total + dot(pair, all_ref[h, 0:128, :])
    first = used[0] * (total[0:64] + const_sum[0:1] + local_ref[128:129, :])
    second = used[1] * (total[64:128] + const_sum[1:2] + local_ref[128:129, :])
    moved = jnp.where(left, second, first)
    for g in range(moved_ref.shape[0]):
        moved_ref[g] = moved.astype(BF16)
    for i, part in ((0, moved[:, 64:128]), (1, moved[:, 0:64])):
        noisy = noisy_latent(level[i], prev_ref[i], noise_ref[i])
        prediction_ref[0, i] = gen * gen_ref[i].astype(F32) + (1.0 - gen) * noisy - part


def guidance(moved_ref):
    return 2.5 * moved_ref[1].astype(F32) - 1.5 * moved_ref[2].astype(F32)


def partial_kernel(group_ref, t_ref, moved_ref, noise_ref, prev_ref, saved_ref, out_ref):
    guided = guidance(moved_ref)
    down = moved_ref[3].astype(F32) - guided
    halves = (slice(64, 128), slice(0, 64))
    row = lax.broadcasted_iota(jnp.int32, (16, 128), 0)
    sums = []
    for i in range(2):
        level = (t_ref[i].astype(F32) + 0.5) * (1.0 / NOISE_LEVEL_COUNT)
        real = noisy_latent(level, prev_ref[i], noise_ref[i]) - guided[:, halves[i]]
        gap = jnp.abs(prev_ref[i] - real)
        sums.append(jnp.sum(jnp.sum(gap, axis=0, keepdims=True), axis=1, keepdims=True))
    sums = jnp.where(row < 8, sums[0], sums[1])
    high = sums.astype(BF16).astype(F32)
    sums = jnp.where(left_half((16, 128)), high, sums - high).astype(BF16)
    tokens = jnp.concatenate([down[:, halves[0]], down[:, halves[1]]], axis=0).astype(BF16)
    out_row = lax.broadcasted_iota(jnp.int32, (128, 64), 0)
    channel = lax.broadcasted_iota(jnp.int32, (128, 64), 1)
    pick = jnp.where((out_row // 16) * 8 + out_row % 8 == channel, 1.0, 0.0).astype(BF16)
    spread_out = dot(pick, tokens, 1, 1)
    image = (lax.broadcasted_iota(jnp.int32, (128, 128), 0) % 16) // 8
    owner = lax.broadcasted_iota(jnp.int32, (128, 128), 1) // 64
    spread_out = jnp.where(image == owner, spread_out, 0.0).astype(BF16)
    saved = jnp.concatenate([saved_ref[0], saved_ref[1]], axis=0)
    grad = dot(spread_out, saved).astype(BF16)
    for a in range(8):
        for b in range(2):
            out_ref[2 * a + b, :, 0:384] = grad[16 * a : 16 * a + 16, 384 * b : 384 * b + 384]
            out_ref[2 * a + b, :, 384:512] = sums


def scale_kernel(factor, part_ref, moved_ref, out_ref, grad_ref):
    total = part_ref[0].astype(F32)
    for s in range(1, part_ref.shape[0]):
        total = total + part_ref[s].astype(F32)
    spread = (total[:, 384:385] + total[:, 448:449]) * (1.0 / (NTOK * 64)) + 1e-05
    grad = total[:, 0:384] * (factor / spread)
    grad = grad[0:8] + grad[8:16]
    for k in range(out_ref.shape[0]):
        out_ref[k] = grad
    gap = guidance(moved_ref) - moved_ref[3].astype(F32)
    grad_ref[0] = gap[:, 64:128] / spread[0:1]
    grad_ref[1] = gap[:, 0:64] / spread[8:9]


def sum_kernel(copies, part_ref, out_ref):
    for g in range(part_ref.shape[0] // copies):
        total = part_ref[g * copies]
        for d in range(1, copies):
            total = total + part_ref[g * copies + d]
        out_ref[:, 384 * g : 384 * g + 384] = total


def place_kernel(part_ref, out_ref):
    for a in range(8):
        for b in range(2):
            for g in range(4):
                out_ref[8 * a : 8 * a + 8, 768 * g + 384 * b : 768 * g + 384 * b + 384] = part_ref[
                    2 * a + b, :, 384 * g : 384 * g + 384
                ]


SCALAR = pl.BlockSpec(memory_space=pltpu.SMEM)
VECTOR = pl.BlockSpec(memory_space=pltpu.VMEM)


def params(mib):
    return pltpu.CompilerParams(vmem_limit_bytes=mib << 20)


def shape_of(shape, dtype):
    return jax.ShapeDtypeStruct(shape, dtype)


def per_device(
    noise_gen,
    noise_score,
    prev_latents,
    t_idx,
    w_in,
    w_qkv,
    w_out,
    w_final,
    mod_scale,
    mod_shift,
    saved_features,
):
    groups = lax.axis_size("group")
    heads = lax.axis_size("seq")
    copies = lax.axis_size("dp")
    group = lax.axis_index("group").astype(jnp.int32).reshape(1)
    width = w_in.shape[2]

    sent, local = pl.pallas_call(
        fold_kernel,
        out_shape=(shape_of((ROWS, 128), BF16), shape_of((136, 128), F32)),
        in_specs=[SCALAR] * 2 + [VECTOR] * 9,
        out_specs=(VECTOR, VECTOR),
        scratch_shapes=[pltpu.VMEM((144, width), BF16)],
        compiler_params=params(24),
        name="fold",
    )(
        group, t_idx, noise_gen, noise_score, prev_latents, w_in,
        w_qkv[0].transpose(1, 0, 2), w_out[0].T, w_final[0].T, mod_scale, mod_shift,
    )
    everyone = lax.all_gather(sent, "seq", axis=0, tiled=True).reshape(heads, ROWS, 128)

    moved, prediction = pl.pallas_call(
        attend_kernel,
        out_shape=(shape_of((groups, 64, 128), BF16), shape_of((1, 2, 64, 64), F32)),
        in_specs=[SCALAR] * 2 + [VECTOR] * 6,
        out_specs=(VECTOR, VECTOR),
        scratch_shapes=[
            pltpu.VMEM((64 * heads, 256), BF16),
            pltpu.VMEM((2, 64 * heads, 128), BF16),
            pltpu.VMEM((2, 64 * heads, 128), BF16),
        ],
        compiler_params=params(32),
        name="attend",
    )(group, t_idx, noise_gen, noise_score, prev_latents, everyone, sent, local)
    moved = lax.all_to_all(moved, "group", 0, 0, tiled=True)

    quarter = width // groups
    whole = lambda *dims: pl.BlockSpec(dims, lambda n, g, t: (0,) * len(dims))
    parts = pl.pallas_call(
        partial_kernel,
        out_shape=shape_of((heads, 16, 512), BF16),
        grid_spec=pltpu.PrefetchScalarGridSpec(
            num_scalar_prefetch=2,
            grid=(1,),
            in_specs=[
                whole(groups, 64, 128),
                whole(2, 64, 64),
                whole(2, 64, 64),
                pl.BlockSpec((2, 64, quarter), lambda n, g, t: (0, 0, g[0])),
            ],
            out_specs=whole(heads, 16, 512),
        ),
        compiler_params=params(16),
        name="partial",
    )(group, t_idx, moved, noise_score, prev_latents, saved_features)
    parts = lax.all_to_all(parts, "seq", 0, 0, tiled=True)

    factor = 1.0 / math.sqrt(2 * copies * NTOK)
    summed, dmd_grad = pl.pallas_call(
        lambda *refs: scale_kernel(factor, *refs),
        out_shape=(shape_of((groups * copies, 8, 384), F32), shape_of((2, 64, 64), F32)),
        in_specs=[VECTOR] * 2,
        out_specs=(VECTOR, VECTOR),
        compiler_params=params(16),
        name="scale",
    )(parts, moved)
    summed = lax.all_to_all(summed, ("group", "dp"), 0, 0, tiled=True)

    rows = pl.pallas_call(
        lambda *refs: sum_kernel(copies, *refs),
        out_shape=shape_of((8, 384 * groups), F32),
        in_specs=[VECTOR],
        out_specs=VECTOR,
        compiler_params=params(16),
        name="sum",
    )(summed)
    rows = lax.all_gather(rows, "seq", axis=0, tiled=True).reshape(heads, 8, 384 * groups)

    total = pl.pallas_call(
        place_kernel,
        out_shape=shape_of((64, width), F32),
        in_specs=[VECTOR],
        out_specs=VECTOR,
        compiler_params=params(16),
        name="place",
    )(rows)
    return prediction, dmd_grad, total.T


def solution(mesh):
    placed = (
        P("dp", "seq", None),
        P("dp", "seq", None),
        P("dp", "seq", None),
        P("dp"),
        P("group", None, None),
        P("group", None, None, "seq"),
        P("group", "seq", None),
        P("group", None, None),
        P("group", None),
        P("group", None),
        P("dp", "seq", None),
    )
    return jax.shard_map(
        per_device,
        mesh=mesh,
        in_specs=placed,
        out_specs=(P("group", "dp", "seq", None), P("dp", "seq", None), P()),
        check_vma=False,
    )
```

time: 1320 us -> 112 us (0.08)
  waiting for transfers between devices: 1240 us -> 0 us
  blocking collectives: 25.7 us -> 92.2 us
  matrix products: 29.3 us -> 0 us
  between operations: 13.9 us -> 0.7 us
    psum x2 -> x0, waiting for transfers between devices: 1100 us -> none  [the longest x1 1050 us: per_device(): total_grad = lax.psum(partial_grad, ('seq', 'dp'))]
    all_gather x1 -> x0, waiting for transfers between devices: 81.5 us -> none  [per_device(): lax.all_gather(features, 'seq', axis=1, tiled=True)]
    reduce_scatter x1 -> x0, waiting for transfers between devices: 55.8 us -> none  [per_device(): lax.psum_scatter(jnp.einsum('sca,af->scf', token_leading_layout, output_l...]
    all_to_all x0 -> x3, blocking collectives: none -> 50.9 us  [the longest x1 18.9 us: per_device(): summed = lax.all_to_all(summed, ('group', 'dp'), 0, 0, tiled=True)]
    all_gather x0 -> x2, blocking collectives: none -> 41.3 us  [the longest x1 23.8 us: per_device(): lax.all_gather(sent, 'seq', axis=0, tiled=True).reshape(heads, ROWS, 128)]
    psum x1 -> x0, blocking collectives: 25.7 us -> none  [per_device(): total_dev = lax.psum(deviation, 'seq')]
    dot_general x5 -> x0, matrix products: 22.1 us -> none  [the longest x1 11.3 us: per_device(): jnp.einsum('ind,de->ine', lax.all_gather(features, 'seq', axis=1, tiled=T...]
  transfers between devices with their start and end apart: 4 -> 0, of which waited for: 4 -> 0; matrix products, arithmetic and copies ran while one was open for 0% -> 0% of each run, Pallas kernels for 0% -> 0%
where the time goes in v1:
time: 112 us; the launch traced here: 111 us
  blocking collectives  92.2 us (82%)
  Pallas kernels  9.2 us (8%)
  local copies, waits for them, and re-layouts  8.81 us (8%)
    all_gather x1, blocking collectives, per_device(): lax.all_gather(sent, 'seq', axis=0, tiled=True).reshape(heads, ROWS, 128)  23.8 us
    all_to_all x1, blocking collectives, per_device(): summed = lax.all_to_all(summed, ('group', 'dp'), 0, 0, tiled=True)  18.9 us
    all_to_all x1, blocking collectives, per_device(): parts = lax.all_to_all(parts, 'seq', 0, 0, tiled=True)  17.6 us
    all_gather x1, blocking collectives, per_device(): lax.all_gather(rows, 'seq', axis=0, tiled=True)  17.5 us
    all_to_all x1, blocking collectives, per_device(): moved = lax.all_to_all(moved, 'group', 0, 0, tiled=True)  14.4 us
    unnamed x30, local copies, waits for them, and re-layouts  8.81 us
    pallas_call x1, Pallas kernels, per_device(): pl.pallas_call(attend_kernel, out_shape=(shape_of((groups, 64, 128), BF16...  4.3 us

profile of v1, /device:TPU:1, one launch (start us, length us, event | category | flops | bytes accessed | tf_op | source)
XLA Modules:
  0.0 110.9 jit_solution(3430302344529975862)
XLA Ops:
  0.6 0.0 copy-start.14
  0.6 0.0 copy-start
  0.7 1.7 %copy-done = bf16[1,3072,3,128]{3,1,2,0:T(8,128)(2,1)S(1)} copy-done((bf16[1,3072,3,128]{3,1,2,0:T(8,128)(2,1)S(1)}, bf16[1,3072,3,128]{3,1,2,0:T(8,128)(2,1)}, u32[]{:S(2)}) %copy-start) | copy-done | bytes 2359320
  2.3 0.0 copy-start.2
  2.3 0.8 copy-done.2
  3.2 0.0 copy-start.4
  3.2 1.0 copy-done.4
  4.2 0.0 copy-start.5
  4.2 1.0 copy-done.5
  5.1 0.0 copy-start.6
  5.2 0.8 copy-done.6
  5.9 0.0 copy-start.8
  5.9 0.8 copy-done.8
  6.7 0.0 copy-start.10
  6.7 0.7 copy-done.10
  7.4 0.0 copy-start.11
  7.4 0.7 copy-done.11
  8.1 0.0 copy-start.12
  8.1 0.7 copy-done.12
  8.8 0.0 copy-start.13
  8.8 0.7 copy-done.13
  9.5 0.0 copy-start.3
  9.5 0.0 copy-start.7
  9.5 0.0 copy-start.9
  9.5 0.0 copy-start.1
  9.5 2.1 %fold.1 = (bf16[208,128]{1,0:T(8,128)(2,1)S(1)}, f32[136,128]{1,0:T(8,128)S(1)}) custom-call(s32[1]{0:T(128)} %bitcast.group_ref, s32[2]{0:T(128)S(1)} %copy-done.13, bf16[2,64,64]{2,1,0:T(8,128)(2,1)S(1)} %copy-done.8, bf16[2,64,64]{2,1,0:T(8,128)(2,1)S(1)} %copy-done.6, f32[2,64,64]{2,1,0:T(8,128)S(1)} %copy-done.2, bf16[1,64,3072]{2,1,0:T(8,128)(2,1)S(1)} %copy-done.4, ...), custom_call_target="tpu_custom_call" | custom-call | tf_op jit(solution)/shard_map/fold/pallas_call | solution.py:244
  11.6 23.8 %all_gather.6 = bf16[3328,128]{1,0:T(8,128)(2,1)S(1)} all-gather(bf16[208,128]{1,0:T(8,128)(2,1)S(1)} %get-tuple-element.9.own_ref), channel_id=1, replica_groups=mesh['group'=4,'seq'=16,'dp'=8] {'seq'}, dimensions={0}, use_global_device_ids=true | all-gather | bytes 905216 | tf_op jit(solution)/shard_map/all_gather | solution.py:256
  35.3 0.0 copy-done.14
  35.4 0.0 copy-done.3
  35.4 0.0 copy-done.7
  35.4 0.0 copy-done.9
  35.4 4.3 %attend.1 = (bf16[4,64,128]{2,1,0:T(8,128)(2,1)S(1)}, f32[1,2,64,64]{3,2,1,0:T(8,128)}) custom-call(s32[1]{0:T(128)} %bitcast.group_ref, s32[2]{0:T(128)S(1)} %copy-done.14, bf16[2,64,64]{2,1,0:T(8,128)(2,1)S(1)} %copy-done.9, bf16[2,64,64]{2,1,0:T(8,128)(2,1)S(1)} %copy-done.7, f32[2,64,64]{2,1,0:T(8,128)S(1)} %copy-done.3, ...), custom_call_target="tpu_custom_call" | custom-call | tf_op jit(solution)/shard_map/attend/pallas_call | solution.py:258
  39.7 14.4 %all_to_all.15.moved_ref.refs_1_ = bf16[4,64,128]{2,1,0:T(8,128)(2,1)S(1)} all-to-all(bf16[4,64,128]{2,1,0:T(8,128)(2,1)S(1)} %get-tuple-element.12), channel_id=1, replica_groups=mesh['group'=4,'seq'=16,'dp'=8] {'group'}, dimensions={0} | all-to-all | bytes 131072 | tf_op jit(solution)/shard_map/all_to_all | solution.py:271
  54.1 0.0 copy-done.1
  54.1 1.0 partial.1
  55.1 17.6 %all_to_all.16.refs_0_ = bf16[16,16,512]{2,1,0:T(8,128)(2,1)S(1)} all-to-all(bf16[16,16,512]{2,1,0:T(8,128)(2,1)S(1)} %partial.1), channel_id=1, replica_groups=mesh['group'=4,'seq'=16,'dp'=8] {'seq'}, dimensions={0} | all-to-all | bytes 524288 | tf_op jit(solution)/shard_map/all_to_all | solution.py:292
  72.7 0.8 scale.1
  73.5 18.9 %all_to_all.17.refs_0_ = f32[32,8,384]{2,1,0:T(8,128)S(1)} all-to-all(f32[32,8,384]{2,1,0:T(8,128)S(1)} %get-tuple-element.14), channel_id=1, replica_groups=mesh['group'=4,'seq'=16,'dp'=8] {'group','dp'}, dimensions={0} | all-to-all | bytes 786432 | tf_op jit(solution)/shard_map/all_to_all | solution.py:303
  92.5 17.5 %all_gather.7 = f32[128,1536]{1,0:T(8,128)S(1)} all-gather(f32[8,1536]{1,0:T(8,128)S(1)} %sum.1), channel_id=1, replica_groups=mesh['group'=4,'seq'=16,'dp'=8] {'seq'}, dimensions={0}, use_global_device_ids=true | all-gather | bytes 835584 | tf_op jit(solution)/shard_map/all_gather | solution.py:313
  110.0 0.9 place.1
  (1 shorter events, 0.0 us)
Async XLA Ops:
  0.6 34.7 %copy-start.14 = (s32[2]{0:T(128)S(1)}, s32[2]{0:T(128)}, u32[]{:S(2)}) copy-start(s32[2]{0:T(128)} %t_ref.5) | copy-start | bytes 28
  0.6 1.7 %copy-start = (bf16[1,3072,3,128]{3,1,2,0:T(8,128)(2,1)S(1)}, bf16[1,3072,3,128]{3,1,2,0:T(8,128)(2,1)}, u32[]{:S(2)}) copy-start(bf16[1,3072,3,128]{3,1,2,0:T(8,128)(2,1)} %param.16) | copy-start | bytes 7077892
  2.3 0.8 copy-start.2
  3.2 1.0 copy-start.4
  4.2 1.0 copy-start.5
  5.1 0.8 copy-start.6
  5.9 0.8 copy-start.8
  6.7 0.7 copy-start.10
  7.4 0.7 copy-start.11
  8.1 0.7 copy-start.12
  8.8 0.7 copy-start.13
  9.5 25.9 %copy-start.3 = (f32[2,64,64]{2,1,0:T(8,128)S(1)}, f32[2,64,64]{2,1,0:T(8,128)}, u32[]{:S(2)}) copy-start(f32[2,64,64]{2,1,0:T(8,128)} %prev_ref.5) | copy-start | bytes 98308
  9.5 25.9 %copy-start.7 = (bf16[2,64,64]{2,1,0:T(8,128)(2,1)S(1)}, bf16[2,64,64]{2,1,0:T(8,128)(2,1)}, u32[]{:S(2)}) copy-start(bf16[2,64,64]{2,1,0:T(8,128)(2,1)} %noise_ref.5) | copy-start | bytes 49156
  9.5 25.9 %copy-start.9 = (bf16[2,64,64]{2,1,0:T(8,128)(2,1)S(1)}, bf16[2,64,64]{2,1,0:T(8,128)(2,1)}, u32[]{:S(2)}) copy-start(bf16[2,64,64]{2,1,0:T(8,128)(2,1)} %gen_ref.3) | copy-start | bytes 49156
  9.5 44.6 %copy-start.1 = (bf16[2,64,3072]{2,1,0:T(8,128)(2,1)S(1)}, bf16[2,64,3072]{2,1,0:T(8,128)(2,1)}, u32[]{:S(2)}) copy-start(bf16[2,64,3072]{2,1,0:T(8,128)(2,1)} %saved_ref.1) | copy-start | bytes 2359300

commit v2 on v1

--- a/solution.py
+++ b/solution.py
@@ -32,10 +32,18 @@
     return (1.0 - level) * prev + level * noise.astype(F32)
 
 
-def fold_kernel(
-    group_ref, t_ref, gen_ref, noise_ref, prev_ref, w_in_ref, w_qkv_ref, w_out_ref, w_final_ref,
-    scale_ref, shift_ref, sent_ref, local_ref, left_ref,
-):
+def fold_kernel(group_ref, t_ref, *refs):
+    sources, (sent_ref, local_ref), held = refs[:9], refs[9:11], refs[11:20]
+    left_ref, arrived = refs[20:]
+    loads = [
+        pltpu.make_async_copy(sources[k], held[k], arrived.at[k]) for k in range(len(sources))
+    ]
+    for load in loads:
+        load.start()
+    prev_ref, gen_ref, noise_ref, w_in_ref, scale_ref, shift_ref = held[:6]
+    w_out_ref, w_final_ref, w_qkv_ref = held[6:]
+    for load in loads[:6]:
+        load.wait()
     width = w_in_ref.shape[2]
     gen, level, used = levels(group_ref, t_ref)
     latents = []
@@ -62,6 +70,8 @@
     scaled = (latent.astype(F32) * lax.rsqrt(mean + 1e-06)).astype(BF16)
     sent_ref[144:208, :] = jnp.concatenate([scaled[0:64], scaled[64:128]], axis=1)
 
+    for load in loads[6:]:
+        load.wait()
     folded = [dot(left_ref[...], w_qkv_ref[c]) for c in range(3)]
     final = dot(left_ref[...], w_final_ref[...], 1, 1)
     const = [part[128:129] + part[129:130] for part in folded]
@@ -186,19 +196,22 @@
     spread = (total[:, 384:385] + total[:, 448:449]) * (1.0 / (NTOK * 64)) + 1e-05
     grad = total[:, 0:384] * (factor / spread)
     grad = grad[0:8] + grad[8:16]
-    for k in range(out_ref.shape[0]):
-        out_ref[k] = grad
+    pair = jnp.concatenate([grad, grad], axis=0).astype(BF16)
+    for at in range(0, out_ref.shape[0], 16):
+        out_ref[at : at + 16, :] = pair
     gap = guidance(moved_ref) - moved_ref[3].astype(F32)
     grad_ref[0] = gap[:, 64:128] / spread[0:1]
     grad_ref[1] = gap[:, 0:64] / spread[8:9]
 
 
-def sum_kernel(copies, part_ref, out_ref):
-    for g in range(part_ref.shape[0] // copies):
-        total = part_ref[g * copies]
-        for d in range(1, copies):
-            total = total + part_ref[g * copies + d]
-        out_ref[:, 384 * g : 384 * g + 384] = total
+def sum_kernel(part_ref, out_ref):
+    groups = out_ref.shape[1] // 384
+    rows = part_ref.shape[0] // groups
+    for g in range(groups):
+        total = part_ref[g * rows : g * rows + 16, :].astype(F32)
+        for at in range(g * rows + 16, (g + 1) * rows, 16):
+            total = total + part_ref[at : at + 16, :].astype(F32)
+        out_ref[:, 384 * g : 384 * g + 384] = total[0:8] + total[8:16]
 
 
 def place_kernel(part_ref, out_ref):
@@ -241,18 +254,20 @@
     group = lax.axis_index("group").astype(jnp.int32).reshape(1)
     width = w_in.shape[2]
 
+    operands = (
+        prev_latents, noise_gen, noise_score, w_in, mod_scale, mod_shift,
+        w_out[0].T, w_final[0].T, w_qkv[0].transpose(1, 0, 2),
+    )
     sent, local = pl.pallas_call(
         fold_kernel,
         out_shape=(shape_of((ROWS, 128), BF16), shape_of((136, 128), F32)),
-        in_specs=[SCALAR] * 2 + [VECTOR] * 9,
+        in_specs=[SCALAR] * 2 + [pl.BlockSpec(memory_space=pl.ANY)] * len(operands),
         out_specs=(VECTOR, VECTOR),
-        scratch_shapes=[pltpu.VMEM((144, width), BF16)],
-        compiler_params=params(24),
+        scratch_shapes=[pltpu.VMEM(x.shape, x.dtype) for x in operands]
+        + [pltpu.VMEM((144, width), BF16), pltpu.SemaphoreType.DMA((len(operands),))],
+        compiler_params=params(58),
         name="fold",
-    )(
-        group, t_idx, noise_gen, noise_score, prev_latents, w_in,
-        w_qkv[0].transpose(1, 0, 2), w_out[0].T, w_final[0].T, mod_scale, mod_shift,
-    )
+    )(group, t_idx, *operands)
     everyone = lax.all_gather(sent, "seq", axis=0, tiled=True).reshape(heads, ROWS, 128)
 
     moved, prediction = pl.pallas_call(
@@ -294,7 +309,7 @@
     factor = 1.0 / math.sqrt(2 * copies * NTOK)
     summed, dmd_grad = pl.pallas_call(
         lambda *refs: scale_kernel(factor, *refs),
-        out_shape=(shape_of((groups * copies, 8, 384), F32), shape_of((2, 64, 64), F32)),
+        out_shape=(shape_of((groups * copies * 8, 384), BF16), shape_of((2, 64, 64), F32)),
         in_specs=[VECTOR] * 2,
         out_specs=(VECTOR, VECTOR),
         compiler_params=params(16),
@@ -303,7 +318,7 @@
     summed = lax.all_to_all(summed, ("group", "dp"), 0, 0, tiled=True)
 
     rows = pl.pallas_call(
-        lambda *refs: sum_kernel(copies, *refs),
+        sum_kernel,
         out_shape=shape_of((8, 384 * groups), F32),
         in_specs=[VECTOR],
         out_specs=VECTOR,

time: 112 us -> 104 us (0.929)
  local copies, waits for them, and re-layouts: 8.81 us -> 1.71 us
  blocking collectives: 92.2 us -> 89.4 us
  Pallas kernels: 9.2 us -> 11.9 us
    unnamed x30 -> x14, local copies, waits for them, and re-layouts: 8.81 us -> 1.71 us
    all_to_all x1, blocking collectives: 18.9 us -> 15.8 us  [per_device(): summed = lax.all_to_all(summed, ('group', 'dp'), 0, 0, tiled=True)]
    pallas_call x1, Pallas kernels: 2.11 us -> 4.84 us  [per_device(): pl.pallas_call(fold_kernel, out_shape=(shape_of((ROWS, 128), BF16), shape...]
where the time goes in v2:
time: 104 us
  blocking collectives  89.4 us (86%)
  Pallas kernels  11.9 us (11%)
  local copies, waits for them, and re-layouts  1.71 us (2%)
    all_gather x1, blocking collectives, per_device(): lax.all_gather(sent, 'seq', axis=0, tiled=True).reshape(heads, ROWS, 128)  24.1 us
    all_gather x1, blocking collectives, per_device(): lax.all_gather(rows, 'seq', axis=0, tiled=True)  17.6 us
    all_to_all x1, blocking collectives, per_device(): parts = lax.all_to_all(parts, 'seq', 0, 0, tiled=True)  17.6 us
    all_to_all x1, blocking collectives, per_device(): summed = lax.all_to_all(summed, ('group', 'dp'), 0, 0, tiled=True)  15.8 us
    all_to_all x1, blocking collectives, per_device(): moved = lax.all_to_all(moved, 'group', 0, 0, tiled=True)  14.4 us
    pallas_call x1, Pallas kernels, per_device(): pl.pallas_call(fold_kernel, out_shape=(shape_of((ROWS, 128), BF16), shape...  4.84 us
    pallas_call x1, Pallas kernels, per_device(): pl.pallas_call(attend_kernel, out_shape=(shape_of((groups, 64, 128), BF16...  4.31 us

profile of v2, /device:TPU:1, one launch (start us, length us, event | category | flops | bytes accessed | tf_op | source)
XLA Modules:
  0.0 103.7 jit_solution(13174951768360921896)
XLA Ops:
  0.6 0.0 copy-start.6
  0.6 0.0 copy-start.1
  0.7 0.0 copy-start.2
  0.7 0.0 copy-start.4
  0.7 0.0 copy-start
  0.7 4.8 %fold.1 = (bf16[208,128]{1,0:T(8,128)(2,1)}, f32[136,128]{1,0:T(8,128)}) custom-call(s32[1]{0:T(128)} %bitcast.group_ref, s32[2]{0:T(128)} %t_ref.5, f32[2,64,64]{2,1,0:T(8,128)} %prev_ref.3, bf16[2,64,64]{2,1,0:T(8,128)(2,1)} %gen_ref.1, bf16[2,64,64]{2,1,0:T(8,128)(2,1)} %noise_ref.3, bf16[1,64,3072]{2,1,0:T(8,128)(2,1)} %refs_3_.1, f32[1,3072]{1,0:T(1,128)} %refs_4_.1, ...), custom_call_target="tpu_custom_call" | custom-call | tf_op jit(solution)/shard_map/fold/pallas_call | solution.py:261
  5.5 24.1 %all_gather.6 = bf16[3328,128]{1,0:T(8,128)(2,1)S(1)} all-gather(bf16[208,128]{1,0:T(8,128)(2,1)} %get-tuple-element.9.own_ref), channel_id=1, replica_groups=mesh['group'=4,'seq'=16,'dp'=8] {'seq'}, dimensions={0}, use_global_device_ids=true | all-gather | bytes 905216 | tf_op jit(solution)/shard_map/all_gather | solution.py:271
  29.6 0.0 copy-done.6
  29.6 0.0 copy-done.1
  29.6 0.0 copy-done.2
  29.6 0.0 copy-done.4
  29.6 0.0 copy-start.3
  29.6 0.8 copy-done.3
  30.4 0.0 copy-start.5
  30.4 0.9 copy-done.5
  31.3 4.3 %attend.1 = (bf16[4,64,128]{2,1,0:T(8,128)(2,1)S(1)}, f32[1,2,64,64]{3,2,1,0:T(8,128)}) custom-call(s32[1]{0:T(128)} %bitcast.group_ref, s32[2]{0:T(128)S(1)} %copy-done.6, bf16[2,64,64]{2,1,0:T(8,128)(2,1)S(1)} %copy-done.4, bf16[2,64,64]{2,1,0:T(8,128)(2,1)S(1)} %copy-done.2, f32[2,64,64]{2,1,0:T(8,128)S(1)} %copy-done.1, ...), custom_call_target="tpu_custom_call" | custom-call | tf_op jit(solution)/shard_map/attend/pallas_call | solution.py:273
  35.6 14.4 %all_to_all.21.moved_ref.refs_1_ = bf16[4,64,128]{2,1,0:T(8,128)(2,1)S(1)} all-to-all(bf16[4,64,128]{2,1,0:T(8,128)(2,1)S(1)} %get-tuple-element.12), channel_id=1, replica_groups=mesh['group'=4,'seq'=16,'dp'=8] {'group'}, dimensions={0} | all-to-all | bytes 131072 | tf_op jit(solution)/shard_map/all_to_all | solution.py:286
  50.0 0.0 copy-done
  50.0 1.0 partial.1
  51.0 17.6 %all_to_all.22.refs_0_ = bf16[16,16,512]{2,1,0:T(8,128)(2,1)S(1)} all-to-all(bf16[16,16,512]{2,1,0:T(8,128)(2,1)S(1)} %partial.1), channel_id=1, replica_groups=mesh['group'=4,'seq'=16,'dp'=8] {'seq'}, dimensions={0} | all-to-all | bytes 524288 | tf_op jit(solution)/shard_map/all_to_all | solution.py:307
  68.6 0.8 scale.1
  69.4 15.8 %all_to_all.23 = bf16[32,8,384]{2,1,0:T(8,128)(2,1)S(1)} all-to-all(bf16[32,8,384]{2,1,0:T(8,128)(2,1)S(1)} %bitcast.18), channel_id=1, replica_groups=mesh['group'=4,'seq'=16,'dp'=8] {'group','dp'}, dimensions={0} | all-to-all | bytes 393216 | tf_op jit(solution)/shard_map/all_to_all | solution.py:318
  85.3 17.6 %all_gather.7 = f32[128,1536]{1,0:T(8,128)S(1)} all-gather(f32[8,1536]{1,0:T(8,128)S(1)} %sum.1), channel_id=1, replica_groups=mesh['group'=4,'seq'=16,'dp'=8] {'seq'}, dimensions={0}, use_global_device_ids=true | all-gather | bytes 835584 | tf_op jit(solution)/shard_map/all_gather | solution.py:328
  102.8 0.9 place.1
  (1 shorter events, 0.0 us)
Async XLA Ops:
  0.6 29.0 %copy-start.6 = (s32[2]{0:T(128)S(1)}, s32[2]{0:T(128)}, u32[]{:S(2)}) copy-start(s32[2]{0:T(128)} %t_ref.5) | copy-start | bytes 28
  0.6 29.0 %copy-start.1 = (f32[2,64,64]{2,1,0:T(8,128)S(1)}, f32[2,64,64]{2,1,0:T(8,128)}, u32[]{:S(2)}) copy-start(f32[2,64,64]{2,1,0:T(8,128)} %prev_ref.3) | copy-start | bytes 98308
  0.7 29.0 %copy-start.2 = (bf16[2,64,64]{2,1,0:T(8,128)(2,1)S(1)}, bf16[2,64,64]{2,1,0:T(8,128)(2,1)}, u32[]{:S(2)}) copy-start(bf16[2,64,64]{2,1,0:T(8,128)(2,1)} %noise_ref.3) | copy-start | bytes 49156
  0.7 29.0 %copy-start.4 = (bf16[2,64,64]{2,1,0:T(8,128)(2,1)S(1)}, bf16[2,64,64]{2,1,0:T(8,128)(2,1)}, u32[]{:S(2)}) copy-start(bf16[2,64,64]{2,1,0:T(8,128)(2,1)} %gen_ref.1) | copy-start | bytes 49156
  0.7 49.3 %copy-start = (bf16[2,64,3072]{2,1,0:T(8,128)(2,1)S(1)}, bf16[2,64,3072]{2,1,0:T(8,128)(2,1)}, u32[]{:S(2)}) copy-start(bf16[2,64,3072]{2,1,0:T(8,128)(2,1)} %saved_ref.1) | copy-start | bytes 2359300
  29.6 0.8 copy-start.3
  30.4 0.9 copy-start.5

commit v3 on v2

--- a/solution.py
+++ b/solution.py
@@ -11,6 +11,7 @@
 NOISE_LEVEL_COUNT = 1000
 BF16 = jnp.bfloat16
 F32 = jnp.float32
+CHUNKS = 3
 ROWS = 208
 
 
@@ -35,45 +36,53 @@
 def fold_kernel(group_ref, t_ref, *refs):
     sources, (sent_ref, local_ref), held = refs[:9], refs[9:11], refs[11:20]
     left_ref, arrived = refs[20:]
-    loads = [
-        pltpu.make_async_copy(sources[k], held[k], arrived.at[k]) for k in range(len(sources))
-    ]
+    width = sources[3].shape[2]
+    step = width // CHUNKS
+    pairs = [(sources[k], held[k]) for k in (0, 1, 2, 4, 5, 6)]
+    for at in range(0, width, step):
+        part = pl.ds(at, step)
+        pairs.append((sources[3].at[:, :, part], held[3].at[:, :, part]))
+        pairs.append((sources[7].at[:, part], held[7].at[:, part]))
+        pairs += [(sources[8].at[c, part], held[8].at[c, part]) for c in range(3)]
+    loads = [pltpu.make_async_copy(*pair, arrived.at[k]) for k, pair in enumerate(pairs)]
     for load in loads:
         load.start()
     prev_ref, gen_ref, noise_ref, w_in_ref, scale_ref, shift_ref = held[:6]
     w_out_ref, w_final_ref, w_qkv_ref = held[6:]
     for load in loads[:6]:
         load.wait()
-    width = w_in_ref.shape[2]
     gen, level, used = levels(group_ref, t_ref)
     latents = []
     for i in range(2):
         noisy = noisy_latent(level[i], prev_ref[i], noise_ref[i])
         latents.append(gen * gen_ref[i].astype(F32) + (1.0 - gen) * noisy)
     latent = jnp.concatenate(latents, axis=0).astype(BF16)
-    step = 512
-    squares = jnp.zeros((128, step), F32)
-    for at in range(0, width, step):
+    squares = jnp.zeros((128, 128), F32)
+    final = jnp.zeros((144, 64), F32)
+    folded = [jnp.zeros((144, 128), F32) for _ in range(3)]
+    row = lax.broadcasted_iota(jnp.int32, (16, step), 0)
+    for n in range(CHUNKS):
+        at = n * step
+        for load in loads[6 + 5 * n : 11 + 5 * n]:
+            load.wait()
         part = w_in_ref[0, :, at : at + step]
         projected = dot(latent, part)
-        squares = squares + projected * projected
-        scale = scale_ref[:, at : at + step]
+        for lane in range(0, step, 128):
+            piece = projected[:, lane : lane + 128]
+            squares = squares + piece * piece
         shift = shift_ref[:, at : at + step]
         high = shift.astype(BF16).astype(F32)
-        row = lax.broadcasted_iota(jnp.int32, (16, step), 0)
-        left_ref[0:64, at : at + step] = part
-        left_ref[64:128, at : at + step] = (part.astype(F32) * scale).astype(BF16)
-        left_ref[128:144, at : at + step] = jnp.where(
-            row == 0, high, jnp.where(row == 1, shift - high, 0.0)
-        ).astype(BF16)
+        shifts = jnp.where(row == 0, high, jnp.where(row == 1, shift - high, 0.0))
+        scaled = part.astype(F32) * scale_ref[:, at : at + step]
+        left_ref[0:64, :] = part
+        left_ref[64:128, :] = scaled.astype(BF16)
+        left_ref[128:144, :] = shifts.astype(BF16)
+        final = final + dot(left_ref[...], w_final_ref[:, at : at + step], 1, 1)
+        for c in range(3):
+            folded[c] = folded[c] + dot(left_ref[...], w_qkv_ref[c, at : at + step, :])
     mean = jnp.sum(squares, axis=1, keepdims=True) * (1.0 / width)
     scaled = (latent.astype(F32) * lax.rsqrt(mean + 1e-06)).astype(BF16)
     sent_ref[144:208, :] = jnp.concatenate([scaled[0:64], scaled[64:128]], axis=1)
-
-    for load in loads[6:]:
-        load.wait()
-    folded = [dot(left_ref[...], w_qkv_ref[c]) for c in range(3)]
-    final = dot(left_ref[...], w_final_ref[...], 1, 1)
     const = [part[128:129] + part[129:130] for part in folded]
     final_const = final[128:129] + final[129:130]
     factor = math.log2(math.e) / math.sqrt(128.0)
@@ -107,16 +116,18 @@
 
 
 def attend_kernel(
-    group_ref, t_ref, gen_ref, noise_ref, prev_ref, all_ref, own_ref, local_ref,
-    moved_ref, prediction_ref, keys_ref, query_ref, mixed_ref,
+    group_ref, me_ref, t_ref, gen_ref, noise_ref, prev_ref, all_ref, local_source,
+    moved_ref, prediction_ref, keys_ref, query_ref, mixed_ref, local_ref, arrived,
 ):
+    load = pltpu.make_async_copy(local_source, local_ref, arrived)
+    load.start()
     heads = all_ref.shape[0]
     gen, level, used = levels(group_ref, t_ref)
     for s in range(heads):
         keys_ref[64 * s : 64 * s + 64, 0:128] = all_ref[s, 144:208, :]
     keys_ref[:, 128:256] = jnp.ones((64 * heads, 128), BF16)
     left = left_half((64, 128))
-    own = own_ref[144:208, :].astype(F32)
+    own = all_ref[me_ref[0], 144:208, :].astype(F32)
     stacked = jnp.concatenate([jnp.where(left, own, 0.0), jnp.where(left, 0.0, own)], axis=0)
     stacked = stacked.astype(BF16)
     const_sum = jnp.zeros((16, 128), F32)
@@ -140,6 +151,7 @@
             mixed = mixed[:, 0:128] / mixed[:, 128:256]
             keep = wide_left if i == 0 else jnp.logical_not(wide_left)
             mixed_ref[i, rows, :] = jnp.where(keep, mixed, 0.0).astype(BF16)
+    load.wait()
     total = dot(stacked, local_ref[0:128, :].astype(BF16))
     for h in range(heads):
         rows = slice(64 * h, 64 * h + 64)
@@ -235,6 +247,39 @@
     return jax.ShapeDtypeStruct(shape, dtype)
 
 
+def fold(group, t_idx, *operands):
+    width = operands[3].shape[2]
+    return pl.pallas_call(
+        fold_kernel,
+        out_shape=(shape_of((ROWS, 128), BF16), pltpu.VMEM((136, 128), F32)),
+        in_specs=[SCALAR] * 2 + [pl.BlockSpec(memory_space=pl.ANY)] * len(operands),
+        out_specs=(VECTOR, VECTOR),
+        scratch_shapes=[pltpu.VMEM(x.shape, x.dtype) for x in operands]
+        + [pltpu.VMEM((144, width // CHUNKS), BF16), pltpu.SemaphoreType.DMA((6 + 5 * CHUNKS,))],
+        compiler_params=params(58),
+        name="fold",
+    )(group, t_idx, *operands)
+
+
+def attend(groups, group, me, t_idx, noise_gen, noise_score, prev_latents, everyone, local):
+    heads = everyone.shape[0]
+    return pl.pallas_call(
+        attend_kernel,
+        out_shape=(shape_of((groups, 64, 128), BF16), shape_of((1, 2, 64, 64), F32)),
+        in_specs=[SCALAR] * 3 + [VECTOR] * 4 + [pl.BlockSpec(memory_space=pl.ANY)],
+        out_specs=(VECTOR, VECTOR),
+        scratch_shapes=[
+            pltpu.VMEM((64 * heads, 256), BF16),
+            pltpu.VMEM((2, 64 * heads, 128), BF16),
+            pltpu.VMEM((2, 64 * heads, 128), BF16),
+            pltpu.VMEM(local.shape, F32),
+            pltpu.SemaphoreType.DMA,
+        ],
+        compiler_params=params(32),
+        name="attend",
+    )(group, me, t_idx, noise_gen, noise_score, prev_latents, everyone, local)
+
+
 def per_device(
     noise_gen,
     noise_score,
@@ -258,31 +303,13 @@
         prev_latents, noise_gen, noise_score, w_in, mod_scale, mod_shift,
         w_out[0].T, w_final[0].T, w_qkv[0].transpose(1, 0, 2),
     )
-    sent, local = pl.pallas_call(
-        fold_kernel,
-        out_shape=(shape_of((ROWS, 128), BF16), shape_of((136, 128), F32)),
-        in_specs=[SCALAR] * 2 + [pl.BlockSpec(memory_space=pl.ANY)] * len(operands),
-        out_specs=(VECTOR, VECTOR),
-        scratch_shapes=[pltpu.VMEM(x.shape, x.dtype) for x in operands]
-        + [pltpu.VMEM((144, width), BF16), pltpu.SemaphoreType.DMA((len(operands),))],
-        compiler_params=params(58),
-        name="fold",
-    )(group, t_idx, *operands)
+    sent, local = fold(group, t_idx, *operands)
     everyone = lax.all_gather(sent, "seq", axis=0, tiled=True).reshape(heads, ROWS, 128)
 
-    moved, prediction = pl.pallas_call(
-        attend_kernel,
-        out_shape=(shape_of((groups, 64, 128), BF16), shape_of((1, 2, 64, 64), F32)),
-        in_specs=[SCALAR] * 2 + [VECTOR] * 6,
-        out_specs=(VECTOR, VECTOR),
-        scratch_shapes=[
-            pltpu.VMEM((64 * heads, 256), BF16),
-            pltpu.VMEM((2, 64 * heads, 128), BF16),
-            pltpu.VMEM((2, 64 * heads, 128), BF16),
-        ],
-        compiler_params=params(32),
-        name="attend",
-    )(group, t_idx, noise_gen, noise_score, prev_latents, everyone, sent, local)
+    me = lax.axis_index("seq").astype(jnp.int32).reshape(1)
+    moved, prediction = attend(
+        groups, group, me, t_idx, noise_gen, noise_score, prev_latents, everyone, local
+    )
     moved = lax.all_to_all(moved, "group", 0, 0, tiled=True)
 
     quarter = width // groups

time: 104 us -> 103 us (level)
  local copies, waits for them, and re-layouts: 1.71 us -> 0.02 us
    unnamed x14 -> x10, local copies, waits for them, and re-layouts: 1.71 us -> 0.02 us
where the time goes in v3:
time: 103 us; the launch traced here: 102 us
  blocking collectives  89.4 us (87%)
  Pallas kernels  12.3 us (12%)
    all_gather x1, blocking collectives, per_device(): lax.all_gather(sent, 'seq', axis=0, tiled=True).reshape(heads, ROWS, 128)  24.1 us
    all_to_all x1, blocking collectives, per_device(): parts = lax.all_to_all(parts, 'seq', 0, 0, tiled=True)  17.6 us
    all_gather x1, blocking collectives, per_device(): lax.all_gather(rows, 'seq', axis=0, tiled=True)  17.6 us
    all_to_all x1, blocking collectives, per_device(): summed = lax.all_to_all(summed, ('group', 'dp'), 0, 0, tiled=True)  15.8 us
    all_to_all x1, blocking collectives, per_device(): moved = lax.all_to_all(moved, 'group', 0, 0, tiled=True)  14.4 us
    pallas_call x1, Pallas kernels, fold(): pl.pallas_call(fold_kernel, out_shape=(shape_of((ROWS, 128), BF16), pltpu...  4.9 us
    pallas_call x1, Pallas kernels, attend(): pl.pallas_call(attend_kernel, out_shape=(shape_of((groups, 64, 128), BF16...  4.64 us

profile of v3, /device:TPU:1, one launch (start us, length us, event | category | flops | bytes accessed | tf_op | source)
XLA Modules:
  0.0 102.5 jit_solution(13838400557837134307)
XLA Ops:
  0.6 0.0 copy-start.4
  0.6 0.0 copy-start.1
  0.7 0.0 copy-start.2
  0.7 0.0 copy-start.3
  0.7 0.0 copy-start
  0.7 4.9 %fold.1 = (bf16[208,128]{1,0:T(8,128)(2,1)}, f32[136,128]{1,0:T(8,128)S(1)}) custom-call(s32[1]{0:T(128)} %bitcast.group_ref, s32[2]{0:T(128)} %t_ref.5, f32[2,64,64]{2,1,0:T(8,128)} %prev_ref.3, bf16[2,64,64]{2,1,0:T(8,128)(2,1)} %gen_ref.1, bf16[2,64,64]{2,1,0:T(8,128)(2,1)} %noise_ref.3, bf16[1,64,3072]{2,1,0:T(8,128)(2,1)} %refs_3_.1, ...), custom_call_target="tpu_custom_call" | custom-call | tf_op jit(solution)/shard_map/fold/pallas_call | solution.py:252
  5.6 24.1 %all_gather.6 = bf16[3328,128]{1,0:T(8,128)(2,1)S(1)} all-gather(bf16[208,128]{1,0:T(8,128)(2,1)} %get-tuple-element.9), channel_id=1, replica_groups=mesh['group'=4,'seq'=16,'dp'=8] {'seq'}, dimensions={0}, use_global_device_ids=true | all-gather | bytes 905216 | tf_op jit(solution)/shard_map/all_gather | solution.py:307
  29.7 0.0 copy-done.4
  29.7 0.0 copy-done.1
  29.7 0.0 copy-done.2
  29.7 0.0 copy-done.3
  29.7 4.6 %attend.1 = (bf16[4,64,128]{2,1,0:T(8,128)(2,1)S(1)}, f32[1,2,64,64]{3,2,1,0:T(8,128)}) custom-call(s32[1]{0:T(128)} %bitcast.group_ref, s32[1]{0:T(128)} %bitcast.1.me_ref, s32[2]{0:T(128)S(1)} %copy-done.4, bf16[2,64,64]{2,1,0:T(8,128)(2,1)S(1)} %copy-done.3, bf16[2,64,64]{2,1,0:T(8,128)(2,1)S(1)} %copy-done.2, f32[2,64,64]{2,1,0:T(8,128)S(1)} %copy-done.1, ...), custom_call_target="tpu_custom_call" | custom-call | tf_op jit(solution)/shard_map/attend/pallas_call | solution.py:266
  34.3 14.4 %all_to_all.21.moved_ref.refs_1_ = bf16[4,64,128]{2,1,0:T(8,128)(2,1)S(1)} all-to-all(bf16[4,64,128]{2,1,0:T(8,128)(2,1)S(1)} %get-tuple-element.12), channel_id=1, replica_groups=mesh['group'=4,'seq'=16,'dp'=8] {'group'}, dimensions={0} | all-to-all | bytes 131072 | tf_op jit(solution)/shard_map/all_to_all | solution.py:313
  48.7 0.0 copy-done
  48.7 1.0 partial.1
  49.8 17.6 %all_to_all.22.refs_0_ = bf16[16,16,512]{2,1,0:T(8,128)(2,1)S(1)} all-to-all(bf16[16,16,512]{2,1,0:T(8,128)(2,1)S(1)} %partial.1), channel_id=1, replica_groups=mesh['group'=4,'seq'=16,'dp'=8] {'seq'}, dimensions={0} | all-to-all | bytes 524288 | tf_op jit(solution)/shard_map/all_to_all | solution.py:334
  67.3 0.8 scale.1
  68.2 15.8 %all_to_all.23 = bf16[32,8,384]{2,1,0:T(8,128)(2,1)S(1)} all-to-all(bf16[32,8,384]{2,1,0:T(8,128)(2,1)S(1)} %bitcast.19), channel_id=1, replica_groups=mesh['group'=4,'seq'=16,'dp'=8] {'group','dp'}, dimensions={0} | all-to-all | bytes 393216 | tf_op jit(solution)/shard_map/all_to_all | solution.py:345
  84.0 17.6 %all_gather.7 = f32[128,1536]{1,0:T(8,128)S(1)} all-gather(f32[8,1536]{1,0:T(8,128)S(1)} %sum.1), channel_id=1, replica_groups=mesh['group'=4,'seq'=16,'dp'=8] {'seq'}, dimensions={0}, use_global_device_ids=true | all-gather | bytes 835584 | tf_op jit(solution)/shard_map/all_gather | solution.py:355
  101.6 0.9 place.1
  (1 shorter events, 0.0 us)
Async XLA Ops:
  0.6 29.0 %copy-start.4 = (s32[2]{0:T(128)S(1)}, s32[2]{0:T(128)}, u32[]{:S(2)}) copy-start(s32[2]{0:T(128)} %t_ref.5) | copy-start | bytes 28
  0.6 29.0 %copy-start.1 = (f32[2,64,64]{2,1,0:T(8,128)S(1)}, f32[2,64,64]{2,1,0:T(8,128)}, u32[]{:S(2)}) copy-start(f32[2,64,64]{2,1,0:T(8,128)} %prev_ref.3) | copy-start | bytes 98308
  0.7 29.0 %copy-start.2 = (bf16[2,64,64]{2,1,0:T(8,128)(2,1)S(1)}, bf16[2,64,64]{2,1,0:T(8,128)(2,1)}, u32[]{:S(2)}) copy-start(bf16[2,64,64]{2,1,0:T(8,128)(2,1)} %noise_ref.3) | copy-start | bytes 49156
  0.7 29.0 %copy-start.3 = (bf16[2,64,64]{2,1,0:T(8,128)(2,1)S(1)}, bf16[2,64,64]{2,1,0:T(8,128)(2,1)}, u32[]{:S(2)}) copy-start(bf16[2,64,64]{2,1,0:T(8,128)(2,1)} %gen_ref.1) | copy-start | bytes 49156
  0.7 48.1 %copy-start = (bf16[2,64,3072]{2,1,0:T(8,128)(2,1)S(1)}, bf16[2,64,3072]{2,1,0:T(8,128)(2,1)}, u32[]{:S(2)}) copy-start(bf16[2,64,3072]{2,1,0:T(8,128)(2,1)} %saved_ref.1) | copy-start | bytes 2359300

commit v4 on v3

--- a/solution.py
+++ b/solution.py
@@ -217,22 +217,23 @@
 
 
 def sum_kernel(part_ref, out_ref):
-    groups = out_ref.shape[1] // 384
-    rows = part_ref.shape[0] // groups
-    for g in range(groups):
-        total = part_ref[g * rows : g * rows + 16, :].astype(F32)
-        for at in range(g * rows + 16, (g + 1) * rows, 16):
-            total = total + part_ref[at : at + 16, :].astype(F32)
-        out_ref[:, 384 * g : 384 * g + 384] = total[0:8] + total[8:16]
+    total = part_ref[0:16, :].astype(F32)
+    for at in range(16, part_ref.shape[0], 16):
+        total = total + part_ref[at : at + 16, :].astype(F32)
+    total = total[0:8] + total[8:16]
+    pair = jnp.concatenate([total, total], axis=0).astype(BF16)
+    for at in range(0, out_ref.shape[0], 16):
+        out_ref[at : at + 16, :] = pair
 
 
 def place_kernel(part_ref, out_ref):
-    for a in range(8):
-        for b in range(2):
-            for g in range(4):
-                out_ref[8 * a : 8 * a + 8, 768 * g + 384 * b : 768 * g + 384 * b + 384] = part_ref[
-                    2 * a + b, :, 384 * g : 384 * g + 384
-                ]
+    at = 0
+    for core in range(2):
+        for g in range(4):
+            lanes = slice(768 * g + 384 * core, 768 * g + 384 * core + 384)
+            for row in range(0, 64, 16):
+                out_ref[row : row + 16, lanes] = part_ref[at : at + 16, :].astype(F32)
+                at += 16
 
 
 SCALAR = pl.BlockSpec(memory_space=pltpu.SMEM)
@@ -336,23 +337,31 @@
     factor = 1.0 / math.sqrt(2 * copies * NTOK)
     summed, dmd_grad = pl.pallas_call(
         lambda *refs: scale_kernel(factor, *refs),
-        out_shape=(shape_of((groups * copies * 8, 384), BF16), shape_of((2, 64, 64), F32)),
+        out_shape=(shape_of((copies * 8, 384), BF16), shape_of((2, 64, 64), F32)),
         in_specs=[VECTOR] * 2,
         out_specs=(VECTOR, VECTOR),
         compiler_params=params(16),
         name="scale",
     )(parts, moved)
-    summed = lax.all_to_all(summed, ("group", "dp"), 0, 0, tiled=True)
-
+    summed = lax.all_to_all(summed, "dp", 0, 0, tiled=True)
+
+    chips = heads // 2
     rows = pl.pallas_call(
         sum_kernel,
-        out_shape=shape_of((8, 384 * groups), F32),
+        out_shape=shape_of((groups * chips * 8, 384), BF16),
         in_specs=[VECTOR],
         out_specs=VECTOR,
         compiler_params=params(16),
         name="sum",
     )(summed)
-    rows = lax.all_gather(rows, "seq", axis=0, tiled=True).reshape(heads, 8, 384 * groups)
+    same_core = [
+        [g * heads + 2 * y + core for g in range(groups) for y in range(chips)] for core in range(2)
+    ]
+    rows = lax.all_to_all(
+        rows, ("group", "seq"), 0, 0, tiled=True, axis_index_groups=same_core
+    )
+    one_chip = [[2 * y, 2 * y + 1] for y in range(chips)]
+    rows = lax.all_gather(rows, "seq", axis=0, tiled=True, axis_index_groups=one_chip)
 
     total = pl.pallas_call(
         place_kernel,

time: 103 us -> 98.6 us (0.957)
  blocking collectives: 89.4 us -> 85.2 us
    all_gather x1, blocking collectives: 17.6 us -> 4.68 us  [per_device(): lax.all_gather(rows, 'seq', axis=0, tiled=True, axis_index_groups=one_chip)]
    all_to_all x1 -> x2, blocking collectives: 15.8 us -> 24.5 us  [the longest x1 14.8 us: per_device(): lax.all_to_all(rows, ('group', 'seq'), 0, 0, tiled=True, axis_index_group...]
where the time goes in v4:
time: 98.6 us; the launch traced here: 98.3 us
  blocking collectives  85.2 us (86%)
  Pallas kernels  12.3 us (12%)
    all_gather x1, blocking collectives, per_device(): lax.all_gather(sent, 'seq', axis=0, tiled=True).reshape(heads, ROWS, 128)  24.1 us
    all_to_all x1, blocking collectives, per_device(): parts = lax.all_to_all(parts, 'seq', 0, 0, tiled=True)  17.6 us
    all_to_all x1, blocking collectives, per_device(): lax.all_to_all(rows, ('group', 'seq'), 0, 0, tiled=True, axis_index_group...  14.8 us
    all_to_all x1, blocking collectives, per_device(): moved = lax.all_to_all(moved, 'group', 0, 0, tiled=True)  14.4 us
    all_to_all x1, blocking collectives, per_device(): summed = lax.all_to_all(summed, 'dp', 0, 0, tiled=True)  9.65 us
    pallas_call x1, Pallas kernels, fold(): pl.pallas_call(fold_kernel, out_shape=(shape_of((ROWS, 128), BF16), pltpu...  4.9 us
    all_gather x1, blocking collectives, per_device(): lax.all_gather(rows, 'seq', axis=0, tiled=True, axis_index_groups=one_chip)  4.68 us
    pallas_call x1, Pallas kernels, attend(): pl.pallas_call(attend_kernel, out_shape=(shape_of((groups, 64, 128), BF16...  4.64 us

profile of v4, /device:TPU:1, one launch (start us, length us, event | category | flops | bytes accessed | tf_op | source)
XLA Modules:
  0.0 98.3 jit_solution(475409717011459408)
XLA Ops:
  0.6 0.0 copy-start.4
  0.6 0.0 copy-start.1
  0.7 0.0 copy-start.2
  0.7 0.0 copy-start.3
  0.7 0.0 copy-start
  0.7 4.9 %fold.1 = (bf16[208,128]{1,0:T(8,128)(2,1)}, f32[136,128]{1,0:T(8,128)S(1)}) custom-call(s32[1]{0:T(128)} %bitcast.group_ref, s32[2]{0:T(128)} %t_ref.5, f32[2,64,64]{2,1,0:T(8,128)} %prev_ref.3, bf16[2,64,64]{2,1,0:T(8,128)(2,1)} %gen_ref.1, bf16[2,64,64]{2,1,0:T(8,128)(2,1)} %noise_ref.3, bf16[1,64,3072]{2,1,0:T(8,128)(2,1)} %refs_3_.1, ...), custom_call_target="tpu_custom_call" | custom-call | tf_op jit(solution)/shard_map/fold/pallas_call | solution.py:253
  5.6 24.1 %all_gather.6 = bf16[3328,128]{1,0:T(8,128)(2,1)S(1)} all-gather(bf16[208,128]{1,0:T(8,128)(2,1)} %get-tuple-element.9), channel_id=1, replica_groups=mesh['group'=4,'seq'=16,'dp'=8] {'seq'}, dimensions={0}, use_global_device_ids=true | all-gather | bytes 905216 | tf_op jit(solution)/shard_map/all_gather | solution.py:308
  29.7 0.0 copy-done.4
  29.7 0.0 copy-done.1
  29.7 0.0 copy-done.2
  29.7 0.0 copy-done.3
  29.7 4.6 %attend.1 = (bf16[4,64,128]{2,1,0:T(8,128)(2,1)S(1)}, f32[1,2,64,64]{3,2,1,0:T(8,128)}) custom-call(s32[1]{0:T(128)} %bitcast.group_ref, s32[1]{0:T(128)} %bitcast.1.me_ref, s32[2]{0:T(128)S(1)} %copy-done.4, bf16[2,64,64]{2,1,0:T(8,128)(2,1)S(1)} %copy-done.3, bf16[2,64,64]{2,1,0:T(8,128)(2,1)S(1)} %copy-done.2, f32[2,64,64]{2,1,0:T(8,128)S(1)} %copy-done.1, ...), custom_call_target="tpu_custom_call" | custom-call | tf_op jit(solution)/shard_map/attend/pallas_call | solution.py:267
  34.3 14.4 %all_to_all.33.moved_ref.refs_1_ = bf16[4,64,128]{2,1,0:T(8,128)(2,1)S(1)} all-to-all(bf16[4,64,128]{2,1,0:T(8,128)(2,1)S(1)} %get-tuple-element.12), channel_id=1, replica_groups=mesh['group'=4,'seq'=16,'dp'=8] {'group'}, dimensions={0} | all-to-all | bytes 131072 | tf_op jit(solution)/shard_map/all_to_all | solution.py:314
  48.7 0.0 copy-done
  48.7 1.0 %partial.1 = bf16[16,16,512]{2,1,0:T(8,128)(2,1)S(1)} custom-call(s32[1]{0:T(128)} %bitcast.group_ref, s32[2]{0:T(128)S(1)} %copy-done.4, bf16[4,64,128]{2,1,0:T(8,128)(2,1)S(1)} %all_to_all.33.moved_ref.refs_1_, bf16[2,64,64]{2,1,0:T(8,128)(2,1)S(1)} %copy-done.2, f32[2,64,64]{2,1,0:T(8,128)S(1)} %copy-done.1, bf16[2,64,3072]{2,1,0:T(8,128)(2,1)S(1)} %copy-done), custom_call_target="tpu_custom_call" | custom-call | tf_op jit(solution)/shard_map/partial/pallas_call | solution.py:318
  49.8 17.6 %all_to_all.34.refs_0_ = bf16[16,16,512]{2,1,0:T(8,128)(2,1)S(1)} all-to-all(bf16[16,16,512]{2,1,0:T(8,128)(2,1)S(1)} %partial.1), channel_id=1, replica_groups=mesh['group'=4,'seq'=16,'dp'=8] {'seq'}, dimensions={0} | all-to-all | bytes 524288 | tf_op jit(solution)/shard_map/all_to_all | solution.py:335
  67.3 0.8 scale.1
  68.2 9.6 %all_to_all.35 = bf16[8,8,384]{2,1,0:T(8,128)(2,1)S(1)} all-to-all(bf16[8,8,384]{2,1,0:T(8,128)(2,1)S(1)} %bitcast.20), channel_id=1, replica_groups=mesh['group'=4,'seq'=16,'dp'=8] {'dp'}, dimensions={0} | all-to-all | bytes 98304 | tf_op jit(solution)/shard_map/all_to_all | solution.py:346
  77.8 14.8 %all_to_all.36 = bf16[32,8,384]{2,1,0:T(8,128)(2,1)S(1)} all-to-all(bf16[32,8,384]{2,1,0:T(8,128)(2,1)S(1)} %bitcast.18), channel_id=1, replica_groups={{0,16,32,48,64,80,96,112,128,144,160,176,192,208,224,240,256,272,288,30..., dimensions={0} | all-to-all | bytes 393216 | tf_op jit(solution)/shard_map/all_to_all | solution.py:360
  92.7 4.7 %all_gather.7.part_ref = bf16[512,384]{1,0:T(8,128)(2,1)S(1)} all-gather(bf16[256,384]{1,0:T(8,128)(2,1)S(1)} %bitcast.23), channel_id=1, replica_groups={{0,8},{16,24},{32,40},{48,56},{64,72},{80,88},{96,104},{112,120},{1,9},..., dimensions={0}, use_global_device_ids=true | all-gather | bytes 589824 | tf_op jit(solution)/shard_map/all_gather | solution.py:364
  97.4 0.9 place.1
  (1 shorter events, 0.0 us)
Async XLA Ops:
  0.6 29.0 %copy-start.4 = (s32[2]{0:T(128)S(1)}, s32[2]{0:T(128)}, u32[]{:S(2)}) copy-start(s32[2]{0:T(128)} %t_ref.5) | copy-start | bytes 28
  0.6 29.0 %copy-start.1 = (f32[2,64,64]{2,1,0:T(8,128)S(1)}, f32[2,64,64]{2,1,0:T(8,128)}, u32[]{:S(2)}) copy-start(f32[2,64,64]{2,1,0:T(8,128)} %prev_ref.3) | copy-start | bytes 98308
  0.7 29.0 %copy-start.2 = (bf16[2,64,64]{2,1,0:T(8,128)(2,1)S(1)}, bf16[2,64,64]{2,1,0:T(8,128)(2,1)}, u32[]{:S(2)}) copy-start(bf16[2,64,64]{2,1,0:T(8,128)(2,1)} %noise_ref.3) | copy-start | bytes 49156
  0.7 29.0 %copy-start.3 = (bf16[2,64,64]{2,1,0:T(8,128)(2,1)S(1)}, bf16[2,64,64]{2,1,0:T(8,128)(2,1)}, u32[]{:S(2)}) copy-start(bf16[2,64,64]{2,1,0:T(8,128)(2,1)} %gen_ref.1) | copy-start | bytes 49156
  0.7 48.1 %copy-start = (bf16[2,64,3072]{2,1,0:T(8,128)(2,1)S(1)}, bf16[2,64,3072]{2,1,0:T(8,128)(2,1)}, u32[]{:S(2)}) copy-start(bf16[2,64,3072]{2,1,0:T(8,128)(2,1)} %saved_ref.1) | copy-start | bytes 2359300

commit v5 on v4

--- a/solution.py
+++ b/solution.py
@@ -23,22 +23,28 @@
     return lax.broadcasted_iota(jnp.int32, shape, 1) < 64
 
 
-def levels(group_ref, t_ref):
-    gen = jnp.where(group_ref[0] == 0, 1.0, 0.0).astype(F32)
+def levels(t_ref):
+    gen = jnp.where(lax.axis_index("group") == 0, 1.0, 0.0).astype(F32)
     level = [(t_ref[i].astype(F32) + 0.5) * (1.0 / NOISE_LEVEL_COUNT) for i in range(2)]
     return gen, level, [gen + (1.0 - gen) * value for value in level]
 
 
+def level_rows(local_ref, lanes):
+    rows = [local_ref[k : k + 1, 0:lanes] for k in range(136, 141)]
+    return rows[0], rows[1:3], rows[3:5]
+
+
 def noisy_latent(level, prev, noise):
     return (1.0 - level) * prev + level * noise.astype(F32)
 
 
-def fold_kernel(group_ref, t_ref, *refs):
-    sources, (sent_ref, local_ref), held = refs[:9], refs[9:11], refs[11:20]
-    left_ref, arrived = refs[20:]
+def fold_kernel(*refs):
+    sources, (sent_ref, own_ref, local_ref), held = refs[:10], refs[10:13], refs[13:23]
+    left_ref, arrived = refs[23:]
+    t_ref = held[9]
     width = sources[3].shape[2]
     step = width // CHUNKS
-    pairs = [(sources[k], held[k]) for k in (0, 1, 2, 4, 5, 6)]
+    pairs = [(sources[k], held[k]) for k in (9, 0, 1, 2, 4, 5, 6)]
     for at in range(0, width, step):
         part = pl.ds(at, step)
         pairs.append((sources[3].at[:, :, part], held[3].at[:, :, part]))
@@ -48,10 +54,10 @@
     for load in loads:
         load.start()
     prev_ref, gen_ref, noise_ref, w_in_ref, scale_ref, shift_ref = held[:6]
-    w_out_ref, w_final_ref, w_qkv_ref = held[6:]
-    for load in loads[:6]:
+    w_out_ref, w_final_ref, w_qkv_ref = held[6:9]
+    for load in loads[:7]:
         load.wait()
-    gen, level, used = levels(group_ref, t_ref)
+    gen, level, used = levels(t_ref)
     latents = []
     for i in range(2):
         noisy = noisy_latent(level[i], prev_ref[i], noise_ref[i])
@@ -63,7 +69,7 @@
     row = lax.broadcasted_iota(jnp.int32, (16, step), 0)
     for n in range(CHUNKS):
         at = n * step
-        for load in loads[6 + 5 * n : 11 + 5 * n]:
+        for load in loads[7 + 5 * n : 12 + 5 * n]:
             load.wait()
         part = w_in_ref[0, :, at : at + step]
         projected = dot(latent, part)
@@ -82,7 +88,9 @@
             folded[c] = folded[c] + dot(left_ref[...], w_qkv_ref[c, at : at + step, :])
     mean = jnp.sum(squares, axis=1, keepdims=True) * (1.0 / width)
     scaled = (latent.astype(F32) * lax.rsqrt(mean + 1e-06)).astype(BF16)
-    sent_ref[144:208, :] = jnp.concatenate([scaled[0:64], scaled[64:128]], axis=1)
+    own = jnp.concatenate([scaled[0:64], scaled[64:128]], axis=1)
+    sent_ref[144:208, :] = own
+    own_ref[...] = own
     const = [part[128:129] + part[129:130] for part in folded]
     final_const = final[128:129] + final[129:130]
     factor = math.log2(math.e) / math.sqrt(128.0)
@@ -113,21 +121,21 @@
     local_ref[64:128, :] = locals_[1]
     both = jnp.concatenate([final_const, final_const], axis=1)
     local_ref[128:136, :] = jnp.broadcast_to(both, (8, 128))
+    for k, value in enumerate([gen, *level, *used]):
+        local_ref[136 + k : 137 + k, :] = jnp.full((1, 128), value, F32)
 
 
 def attend_kernel(
-    group_ref, me_ref, t_ref, gen_ref, noise_ref, prev_ref, all_ref, local_source,
-    moved_ref, prediction_ref, keys_ref, query_ref, mixed_ref, local_ref, arrived,
+    gen_ref, noise_ref, prev_ref, all_ref, own_ref, local_ref,
+    moved_ref, prediction_ref, keys_ref, query_ref, mixed_ref,
 ):
-    load = pltpu.make_async_copy(local_source, local_ref, arrived)
-    load.start()
     heads = all_ref.shape[0]
-    gen, level, used = levels(group_ref, t_ref)
+    gen, level, used = level_rows(local_ref, 64)
     for s in range(heads):
         keys_ref[64 * s : 64 * s + 64, 0:128] = all_ref[s, 144:208, :]
     keys_ref[:, 128:256] = jnp.ones((64 * heads, 128), BF16)
     left = left_half((64, 128))
-    own = all_ref[me_ref[0], 144:208, :].astype(F32)
+    own = own_ref[...].astype(F32)
     stacked = jnp.concatenate([jnp.where(left, own, 0.0), jnp.where(left, 0.0, own)], axis=0)
     stacked = stacked.astype(BF16)
     const_sum = jnp.zeros((16, 128), F32)
@@ -151,14 +159,14 @@
             mixed = mixed[:, 0:128] / mixed[:, 128:256]
             keep = wide_left if i == 0 else jnp.logical_not(wide_left)
             mixed_ref[i, rows, :] = jnp.where(keep, mixed, 0.0).astype(BF16)
-    load.wait()
     total = dot(stacked, local_ref[0:128, :].astype(BF16))
     for h in range(heads):
         rows = slice(64 * h, 64 * h + 64)
         pair = jnp.concatenate([mixed_ref[0, rows, :], mixed_ref[1, rows, :]], axis=0)
         total = total + dot(pair, all_ref[h, 0:128, :])
-    first = used[0] * (total[0:64] + const_sum[0:1] + local_ref[128:129, :])
-    second = used[1] * (total[64:128] + const_sum[1:2] + local_ref[128:129, :])
+    wide = level_rows(local_ref, 128)[2]
+    first = wide[0] * (total[0:64] + const_sum[0:1] + local_ref[128:129, :])
+    second = wide[1] * (total[64:128] + const_sum[1:2] + local_ref[128:129, :])
     moved = jnp.where(left, second, first)
     for g in range(moved_ref.shape[0]):
         moved_ref[g] = moved.astype(BF16)
@@ -171,15 +179,15 @@
     return 2.5 * moved_ref[1].astype(F32) - 1.5 * moved_ref[2].astype(F32)
 
 
-def partial_kernel(group_ref, t_ref, moved_ref, noise_ref, prev_ref, saved_ref, out_ref):
+def partial_kernel(moved_ref, noise_ref, prev_ref, local_ref, saved_ref, out_ref):
+    level = level_rows(local_ref, 64)[1]
     guided = guidance(moved_ref)
     down = moved_ref[3].astype(F32) - guided
     halves = (slice(64, 128), slice(0, 64))
     row = lax.broadcasted_iota(jnp.int32, (16, 128), 0)
     sums = []
     for i in range(2):
-        level = (t_ref[i].astype(F32) + 0.5) * (1.0 / NOISE_LEVEL_COUNT)
-        real = noisy_latent(level, prev_ref[i], noise_ref[i]) - guided[:, halves[i]]
+        real = noisy_latent(level[i], prev_ref[i], noise_ref[i]) - guided[:, halves[i]]
         gap = jnp.abs(prev_ref[i] - real)
         sums.append(jnp.sum(jnp.sum(gap, axis=0, keepdims=True), axis=1, keepdims=True))
     sums = jnp.where(row < 8, sums[0], sums[1])
@@ -193,7 +201,8 @@
     image = (lax.broadcasted_iota(jnp.int32, (128, 128), 0) % 16) // 8
     owner = lax.broadcasted_iota(jnp.int32, (128, 128), 1) // 64
     spread_out = jnp.where(image == owner, spread_out, 0.0).astype(BF16)
-    saved = jnp.concatenate([saved_ref[0], saved_ref[1]], axis=0)
+    lanes = pl.ds(pl.multiple_of(lax.axis_index("group") * 768, 128), 768)
+    saved = jnp.concatenate([saved_ref[0, :, lanes], saved_ref[1, :, lanes]], axis=0)
     grad = dot(spread_out, saved).astype(BF16)
     for a in range(8):
         for b in range(2):
@@ -236,7 +245,6 @@
                 at += 16
 
 
-SCALAR = pl.BlockSpec(memory_space=pltpu.SMEM)
 VECTOR = pl.BlockSpec(memory_space=pltpu.VMEM)
 
 
@@ -248,37 +256,41 @@
     return jax.ShapeDtypeStruct(shape, dtype)
 
 
-def fold(group, t_idx, *operands):
+def fold(*operands):
     width = operands[3].shape[2]
     return pl.pallas_call(
         fold_kernel,
-        out_shape=(shape_of((ROWS, 128), BF16), pltpu.VMEM((136, 128), F32)),
-        in_specs=[SCALAR] * 2 + [pl.BlockSpec(memory_space=pl.ANY)] * len(operands),
-        out_specs=(VECTOR, VECTOR),
-        scratch_shapes=[pltpu.VMEM(x.shape, x.dtype) for x in operands]
-        + [pltpu.VMEM((144, width // CHUNKS), BF16), pltpu.SemaphoreType.DMA((6 + 5 * CHUNKS,))],
+        out_shape=(
+            shape_of((ROWS, 128), BF16), pltpu.VMEM((64, 128), BF16), pltpu.VMEM((144, 128), F32)
+        ),
+        in_specs=[pl.BlockSpec(memory_space=pl.ANY)] * len(operands),
+        out_specs=(VECTOR, VECTOR, VECTOR),
+        scratch_shapes=[pltpu.VMEM(x.shape, x.dtype) for x in operands[:9]]
+        + [
+            pltpu.SMEM(operands[9].shape, jnp.int32),
+            pltpu.VMEM((144, width // CHUNKS), BF16),
+            pltpu.SemaphoreType.DMA((7 + 5 * CHUNKS,)),
+        ],
         compiler_params=params(58),
         name="fold",
-    )(group, t_idx, *operands)
-
-
-def attend(groups, group, me, t_idx, noise_gen, noise_score, prev_latents, everyone, local):
-    heads = everyone.shape[0]
+    )(*operands)
+
+
+def attend(groups, *operands):
+    heads = operands[3].shape[0]
     return pl.pallas_call(
         attend_kernel,
         out_shape=(shape_of((groups, 64, 128), BF16), shape_of((1, 2, 64, 64), F32)),
-        in_specs=[SCALAR] * 3 + [VECTOR] * 4 + [pl.BlockSpec(memory_space=pl.ANY)],
+        in_specs=[VECTOR] * 6,
         out_specs=(VECTOR, VECTOR),
         scratch_shapes=[
             pltpu.VMEM((64 * heads, 256), BF16),
             pltpu.VMEM((2, 64 * heads, 128), BF16),
             pltpu.VMEM((2, 64 * heads, 128), BF16),
-            pltpu.VMEM(local.shape, F32),
-            pltpu.SemaphoreType.DMA,
         ],
         compiler_params=params(32),
         name="attend",
-    )(group, me, t_idx, noise_gen, noise_score, prev_latents, everyone, local)
+    )(*operands)
 
 
 def per_device(
@@ -297,41 +309,27 @@
     groups = lax.axis_size("group")
     heads = lax.axis_size("seq")
     copies = lax.axis_size("dp")
-    group = lax.axis_index("group").astype(jnp.int32).reshape(1)
     width = w_in.shape[2]
 
-    operands = (
+    sent, own, local = fold(
         prev_latents, noise_gen, noise_score, w_in, mod_scale, mod_shift,
-        w_out[0].T, w_final[0].T, w_qkv[0].transpose(1, 0, 2),
-    )
-    sent, local = fold(group, t_idx, *operands)
+        w_out[0].T, w_final[0].T, w_qkv[0].transpose(1, 0, 2), t_idx,
+    )
     everyone = lax.all_gather(sent, "seq", axis=0, tiled=True).reshape(heads, ROWS, 128)
 
-    me = lax.axis_index("seq").astype(jnp.int32).reshape(1)
     moved, prediction = attend(
-        groups, group, me, t_idx, noise_gen, noise_score, prev_latents, everyone, local
+        groups, noise_gen, noise_score, prev_latents, everyone, own, local
     )
     moved = lax.all_to_all(moved, "group", 0, 0, tiled=True)
 
-    quarter = width // groups
-    whole = lambda *dims: pl.BlockSpec(dims, lambda n, g, t: (0,) * len(dims))
     parts = pl.pallas_call(
         partial_kernel,
         out_shape=shape_of((heads, 16, 512), BF16),
-        grid_spec=pltpu.PrefetchScalarGridSpec(
-            num_scalar_prefetch=2,
-            grid=(1,),
-            in_specs=[
-                whole(groups, 64, 128),
-                whole(2, 64, 64),
-                whole(2, 64, 64),
-                pl.BlockSpec((2, 64, quarter), lambda n, g, t: (0, 0, g[0])),
-            ],
-            out_specs=whole(heads, 16, 512),
-        ),
+        in_specs=[VECTOR] * 5,
+        out_specs=VECTOR,
         compiler_params=params(16),
         name="partial",
-    )(group, t_idx, moved, noise_score, prev_latents, saved_features)
+    )(moved, noise_score, prev_latents, local, saved_features)
     parts = lax.all_to_all(parts, "seq", 0, 0, tiled=True)
 
     factor = 1.0 / math.sqrt(2 * copies * NTOK)

time: 98.6 us -> 96.4 us (0.978)
  Pallas kernels: 12.3 us -> 10.2 us
where the time goes in v5:
time: 96.4 us; the launch traced here: 96.1 us
  blocking collectives  85.2 us (88%)
  Pallas kernels  10.2 us (11%)
    all_gather x1, blocking collectives, per_device(): lax.all_gather(sent, 'seq', axis=0, tiled=True).reshape(heads, ROWS, 128)  24.1 us
    all_to_all x1, blocking collectives, per_device(): parts = lax.all_to_all(parts, 'seq', 0, 0, tiled=True)  17.6 us
    all_to_all x1, blocking collectives, per_device(): lax.all_to_all(rows, ('group', 'seq'), 0, 0, tiled=True, axis_index_group...  14.8 us
    all_to_all x1, blocking collectives, per_device(): moved = lax.all_to_all(moved, 'group', 0, 0, tiled=True)  14.4 us
    all_to_all x1, blocking collectives, per_device(): summed = lax.all_to_all(summed, 'dp', 0, 0, tiled=True)  9.64 us
    all_gather x1, blocking collectives, per_device(): lax.all_gather(rows, 'seq', axis=0, tiled=True, axis_index_groups=one_chip)  4.7 us
    pallas_call x1, Pallas kernels, fold(): pl.pallas_call(fold_kernel, out_shape=(shape_of((ROWS, 128), BF16), pltpu...  4.18 us
    pallas_call x1, Pallas kernels, attend(): pl.pallas_call(attend_kernel, out_shape=(shape_of((groups, 64, 128), BF16...  3.78 us

profile of v5, /device:TPU:1, one launch (start us, length us, event | category | flops | bytes accessed | tf_op | source)
XLA Modules:
  0.0 96.1 jit_solution(3134051656695347045)
XLA Ops:
  0.6 0.0 copy-start.1
  0.6 0.0 copy-start.2
  0.7 0.0 copy-start.3
  0.7 0.0 copy-start
  0.7 4.2 %fold.1 = (bf16[208,128]{1,0:T(8,128)(2,1)}, bf16[64,128]{1,0:T(8,128)(2,1)S(1)}, f32[144,128]{1,0:T(8,128)S(1)}) custom-call(f32[2,64,64]{2,1,0:T(8,128)} %prev_ref.3, bf16[2,64,64]{2,1,0:T(8,128)(2,1)} %gen_ref.1, bf16[2,64,64]{2,1,0:T(8,128)(2,1)} %noise_ref.3, bf16[1,64,3072]{2,1,0:T(8,128)(2,1)} %refs_3_.1, f32[1,3072]{1,0:T(1,128)} %refs_4_.1, ...), custom_call_target="tpu_custom_call" | custom-call | tf_op jit(solution)/shard_map/fold/pallas_call | solution.py:261
  4.9 24.1 %all_gather.6 = bf16[3328,128]{1,0:T(8,128)(2,1)S(1)} all-gather(bf16[208,128]{1,0:T(8,128)(2,1)} %get-tuple-element.10), channel_id=1, replica_groups=mesh['group'=4,'seq'=16,'dp'=8] {'seq'}, dimensions={0}, use_global_device_ids=true | all-gather | bytes 905216 | tf_op jit(solution)/shard_map/all_gather | solution.py:318
  28.9 0.0 copy-done.1
  28.9 0.0 copy-done.2
  29.0 0.0 copy-done.3
  29.0 3.8 %attend.1 = (bf16[4,64,128]{2,1,0:T(8,128)(2,1)S(1)}, f32[1,2,64,64]{3,2,1,0:T(8,128)}) custom-call(bf16[2,64,64]{2,1,0:T(8,128)(2,1)S(1)} %copy-done.3, bf16[2,64,64]{2,1,0:T(8,128)(2,1)S(1)} %copy-done.2, f32[2,64,64]{2,1,0:T(8,128)S(1)} %copy-done.1, bf16[16,208,128]{2,1,0:T(8,128)(2,1)S(1)} %bitcast.15, bf16[64,128]{1,0:T(8,128)(2,1)S(1)} %get-tuple-element.11.own_ref, ...), custom_call_target="tpu_custom_call" | custom-call | tf_op jit(solution)/shard_map/attend/pallas_call | solution.py:281
  32.7 14.4 %all_to_all.33.moved_ref.refs_1_ = bf16[4,64,128]{2,1,0:T(8,128)(2,1)S(1)} all-to-all(bf16[4,64,128]{2,1,0:T(8,128)(2,1)S(1)} %get-tuple-element.14), channel_id=1, replica_groups=mesh['group'=4,'seq'=16,'dp'=8] {'group'}, dimensions={0} | all-to-all | bytes 131072 | tf_op jit(solution)/shard_map/all_to_all | solution.py:323
  47.1 0.0 copy-done
  47.1 0.5 partial.1
  47.6 17.6 %all_to_all.34.refs_0_ = bf16[16,16,512]{2,1,0:T(8,128)(2,1)S(1)} all-to-all(bf16[16,16,512]{2,1,0:T(8,128)(2,1)S(1)} %partial.1), channel_id=1, replica_groups=mesh['group'=4,'seq'=16,'dp'=8] {'seq'}, dimensions={0} | all-to-all | bytes 524288 | tf_op jit(solution)/shard_map/all_to_all | solution.py:333
  65.2 0.8 scale.1
  66.0 9.6 %all_to_all.35 = bf16[8,8,384]{2,1,0:T(8,128)(2,1)S(1)} all-to-all(bf16[8,8,384]{2,1,0:T(8,128)(2,1)S(1)} %bitcast.18), channel_id=1, replica_groups=mesh['group'=4,'seq'=16,'dp'=8] {'dp'}, dimensions={0} | all-to-all | bytes 98304 | tf_op jit(solution)/shard_map/all_to_all | solution.py:344
  75.7 14.8 %all_to_all.36 = bf16[32,8,384]{2,1,0:T(8,128)(2,1)S(1)} all-to-all(bf16[32,8,384]{2,1,0:T(8,128)(2,1)S(1)} %bitcast.16), channel_id=1, replica_groups={{0,16,32,48,64,80,96,112,128,144,160,176,192,208,224,240,256,272,288,30..., dimensions={0} | all-to-all | bytes 393216 | tf_op jit(solution)/shard_map/all_to_all | solution.py:358
  90.5 4.7 %all_gather.7.part_ref = bf16[512,384]{1,0:T(8,128)(2,1)S(1)} all-gather(bf16[256,384]{1,0:T(8,128)(2,1)S(1)} %bitcast.21), channel_id=1, replica_groups={{0,8},{16,24},{32,40},{48,56},{64,72},{80,88},{96,104},{112,120},{1,9},..., dimensions={0}, use_global_device_ids=true | all-gather | bytes 589824 | tf_op jit(solution)/shard_map/all_gather | solution.py:362
  95.2 0.9 place.1
  (1 shorter events, 0.0 us)
Async XLA Ops:
  0.6 28.3 %copy-start.1 = (f32[2,64,64]{2,1,0:T(8,128)S(1)}, f32[2,64,64]{2,1,0:T(8,128)}, u32[]{:S(2)}) copy-start(f32[2,64,64]{2,1,0:T(8,128)} %prev_ref.3) | copy-start | bytes 98308
  0.6 28.3 %copy-start.2 = (bf16[2,64,64]{2,1,0:T(8,128)(2,1)S(1)}, bf16[2,64,64]{2,1,0:T(8,128)(2,1)}, u32[]{:S(2)}) copy-start(bf16[2,64,64]{2,1,0:T(8,128)(2,1)} %noise_ref.3) | copy-start | bytes 49156
  0.7 28.3 %copy-start.3 = (bf16[2,64,64]{2,1,0:T(8,128)(2,1)S(1)}, bf16[2,64,64]{2,1,0:T(8,128)(2,1)}, u32[]{:S(2)}) copy-start(bf16[2,64,64]{2,1,0:T(8,128)(2,1)} %gen_ref.1) | copy-start | bytes 49156
  0.7 46.5 %copy-start = (bf16[2,64,3072]{2,1,0:T(8,128)(2,1)S(1)}, bf16[2,64,3072]{2,1,0:T(8,128)(2,1)}, u32[]{:S(2)}) copy-start(bf16[2,64,3072]{2,1,0:T(8,128)(2,1)} %saved_ref.1) | copy-start | bytes 2359300

commit v6 on v5

--- a/solution.py
+++ b/solution.py
@@ -235,14 +235,27 @@
         out_ref[at : at + 16, :] = pair
 
 
-def place_kernel(part_ref, out_ref):
+def place_kernel(
+    part_ref, prediction_ref, grad_ref, out_ref, prediction_out, grad_out, wide_ref, done
+):
+    stores = [
+        pltpu.make_async_copy(prediction_ref, prediction_out, done.at[8]),
+        pltpu.make_async_copy(grad_ref, grad_out, done.at[9]),
+    ]
+    for store in stores:
+        store.start()
     at = 0
     for core in range(2):
         for g in range(4):
-            lanes = slice(768 * g + 384 * core, 768 * g + 384 * core + 384)
+            lanes = pl.ds(768 * g + 384 * core, 384)
             for row in range(0, 64, 16):
-                out_ref[row : row + 16, lanes] = part_ref[at : at + 16, :].astype(F32)
+                wide_ref[row : row + 16, lanes] = part_ref[at : at + 16, :].astype(F32)
                 at += 16
+            source, target = wide_ref.at[:, lanes], out_ref.at[:, lanes]
+            stores.append(pltpu.make_async_copy(source, target, done.at[4 * core + g]))
+            stores[-1].start()
+    for store in stores:
+        store.wait()
 
 
 VECTOR = pl.BlockSpec(memory_space=pltpu.VMEM)
@@ -261,7 +274,7 @@
     return pl.pallas_call(
         fold_kernel,
         out_shape=(
-            shape_of((ROWS, 128), BF16), pltpu.VMEM((64, 128), BF16), pltpu.VMEM((144, 128), F32)
+            pltpu.VMEM((ROWS, 128), BF16), pltpu.VMEM((64, 128), BF16), pltpu.VMEM((144, 128), F32)
         ),
         in_specs=[pl.BlockSpec(memory_space=pl.ANY)] * len(operands),
         out_specs=(VECTOR, VECTOR, VECTOR),
@@ -280,7 +293,7 @@
     heads = operands[3].shape[0]
     return pl.pallas_call(
         attend_kernel,
-        out_shape=(shape_of((groups, 64, 128), BF16), shape_of((1, 2, 64, 64), F32)),
+        out_shape=(shape_of((groups, 64, 128), BF16), pltpu.VMEM((1, 2, 64, 64), F32)),
         in_specs=[VECTOR] * 6,
         out_specs=(VECTOR, VECTOR),
         scratch_shapes=[
@@ -335,7 +348,7 @@
     factor = 1.0 / math.sqrt(2 * copies * NTOK)
     summed, dmd_grad = pl.pallas_call(
         lambda *refs: scale_kernel(factor, *refs),
-        out_shape=(shape_of((copies * 8, 384), BF16), shape_of((2, 64, 64), F32)),
+        out_shape=(shape_of((copies * 8, 384), BF16), pltpu.VMEM((2, 64, 64), F32)),
         in_specs=[VECTOR] * 2,
         out_specs=(VECTOR, VECTOR),
         compiler_params=params(16),
@@ -361,14 +374,17 @@
     one_chip = [[2 * y, 2 * y + 1] for y in range(chips)]
     rows = lax.all_gather(rows, "seq", axis=0, tiled=True, axis_index_groups=one_chip)
 
-    total = pl.pallas_call(
+    total, prediction, dmd_grad = pl.pallas_call(
         place_kernel,
-        out_shape=shape_of((64, width), F32),
-        in_specs=[VECTOR],
-        out_specs=VECTOR,
+        out_shape=(
+            shape_of((64, width), F32), shape_of(prediction.shape, F32), shape_of(dmd_grad.shape, F32)
+        ),
+        in_specs=[VECTOR] * 3,
+        out_specs=(pl.BlockSpec(memory_space=pl.ANY),) * 3,
+        scratch_shapes=[pltpu.VMEM((64, width), F32), pltpu.SemaphoreType.DMA((10,))],
         compiler_params=params(16),
         name="place",
-    )(rows)
+    )(rows, prediction, dmd_grad)
     return prediction, dmd_grad, total.T
 
 

time: 96.4 us -> 94.3 us (0.978)
  Pallas kernels: 10.2 us -> 8.41 us
where the time goes in v6:
time: 94.3 us; the launch traced here: 94.1 us
  blocking collectives  84.9 us (90%)
  Pallas kernels  8.41 us (9%)
    all_gather x1, blocking collectives, per_device(): lax.all_gather(sent, 'seq', axis=0, tiled=True).reshape(heads, ROWS, 128)  23.8 us
    all_to_all x1, blocking collectives, per_device(): parts = lax.all_to_all(parts, 'seq', 0, 0, tiled=True)  17.6 us
    all_to_all x1, blocking collectives, per_device(): lax.all_to_all(rows, ('group', 'seq'), 0, 0, tiled=True, axis_index_group...  14.8 us
    all_to_all x1, blocking collectives, per_device(): moved = lax.all_to_all(moved, 'group', 0, 0, tiled=True)  14.4 us
    all_to_all x1, blocking collectives, per_device(): summed = lax.all_to_all(summed, 'dp', 0, 0, tiled=True)  9.65 us
    all_gather x1, blocking collectives, per_device(): lax.all_gather(rows, 'seq', axis=0, tiled=True, axis_index_groups=one_chip)  4.69 us
    pallas_call x1, Pallas kernels, fold(): pl.pallas_call(fold_kernel, out_shape=(pltpu.VMEM((ROWS, 128), BF16), plt...  3.56 us
    pallas_call x1, Pallas kernels, attend(): pl.pallas_call(attend_kernel, out_shape=(shape_of((groups, 64, 128), BF16...  3.15 us

profile of v6, /device:TPU:1, one launch (start us, length us, event | category | flops | bytes accessed | tf_op | source)
XLA Modules:
  0.0 94.1 jit_solution(8290927727666017564)
XLA Ops:
  0.6 0.0 copy-start.1
  0.6 0.0 copy-start.2
  0.7 0.0 copy-start.3
  0.7 0.0 copy-start
  0.7 3.6 %fold.1 = (bf16[208,128]{1,0:T(8,128)(2,1)S(1)}, bf16[64,128]{1,0:T(8,128)(2,1)S(1)}, f32[144,128]{1,0:T(8,128)S(1)}) custom-call(f32[2,64,64]{2,1,0:T(8,128)} %prev_ref.3, bf16[2,64,64]{2,1,0:T(8,128)(2,1)} %gen_ref.1, bf16[2,64,64]{2,1,0:T(8,128)(2,1)} %noise_ref.3, bf16[1,64,3072]{2,1,0:T(8,128)(2,1)} %refs_3_.1, f32[1,3072]{1,0:T(1,128)} %refs_4_.1, ...), custom_call_target="tpu_custom_call" | custom-call | tf_op jit(solution)/shard_map/fold/pallas_call | solution.py:274
  4.2 23.8 %all_gather.6 = bf16[3328,128]{1,0:T(8,128)(2,1)S(1)} all-gather(bf16[208,128]{1,0:T(8,128)(2,1)S(1)} %get-tuple-element.13), channel_id=1, replica_groups=mesh['group'=4,'seq'=16,'dp'=8] {'seq'}, dimensions={0}, use_global_device_ids=true | all-gather | bytes 905216 | tf_op jit(solution)/shard_map/all_gather | solution.py:331
  28.0 0.0 copy-done.1
  28.0 0.0 copy-done.2
  28.0 0.0 copy-done.3
  28.0 3.2 %attend.1 = (bf16[4,64,128]{2,1,0:T(8,128)(2,1)S(1)}, f32[1,2,64,64]{3,2,1,0:T(8,128)S(1)}) custom-call(bf16[2,64,64]{2,1,0:T(8,128)(2,1)S(1)} %copy-done.3, bf16[2,64,64]{2,1,0:T(8,128)(2,1)S(1)} %copy-done.2, f32[2,64,64]{2,1,0:T(8,128)S(1)} %copy-done.1, bf16[16,208,128]{2,1,0:T(8,128)(2,1)S(1)} %bitcast.15, ...), custom_call_target="tpu_custom_call" | custom-call | tf_op jit(solution)/shard_map/attend/pallas_call | solution.py:294
  31.2 14.4 %all_to_all.33.moved_ref.refs_1_ = bf16[4,64,128]{2,1,0:T(8,128)(2,1)S(1)} all-to-all(bf16[4,64,128]{2,1,0:T(8,128)(2,1)S(1)} %get-tuple-element.16), channel_id=1, replica_groups=mesh['group'=4,'seq'=16,'dp'=8] {'group'}, dimensions={0} | all-to-all | bytes 131072 | tf_op jit(solution)/shard_map/all_to_all | solution.py:336
  45.6 0.0 copy-done
  45.6 0.5 partial.1
  46.1 17.6 %all_to_all.34.refs_0_ = bf16[16,16,512]{2,1,0:T(8,128)(2,1)S(1)} all-to-all(bf16[16,16,512]{2,1,0:T(8,128)(2,1)S(1)} %partial.1), channel_id=1, replica_groups=mesh['group'=4,'seq'=16,'dp'=8] {'seq'}, dimensions={0} | all-to-all | bytes 524288 | tf_op jit(solution)/shard_map/all_to_all | solution.py:346
  63.7 0.2 scale.1
  63.9 9.6 %all_to_all.35 = bf16[8,8,384]{2,1,0:T(8,128)(2,1)S(1)} all-to-all(bf16[8,8,384]{2,1,0:T(8,128)(2,1)S(1)} %bitcast.18), channel_id=1, replica_groups=mesh['group'=4,'seq'=16,'dp'=8] {'dp'}, dimensions={0} | all-to-all | bytes 98304 | tf_op jit(solution)/shard_map/all_to_all | solution.py:357
  73.5 14.8 %all_to_all.36 = bf16[32,8,384]{2,1,0:T(8,128)(2,1)S(1)} all-to-all(bf16[32,8,384]{2,1,0:T(8,128)(2,1)S(1)} %bitcast.16), channel_id=1, replica_groups={{0,16,32,48,64,80,96,112,128,144,160,176,192,208,224,240,256,272,288,30..., dimensions={0} | all-to-all | bytes 393216 | tf_op jit(solution)/shard_map/all_to_all | solution.py:371
  88.4 4.7 %all_gather.7.part_ref = bf16[512,384]{1,0:T(8,128)(2,1)S(1)} all-gather(bf16[256,384]{1,0:T(8,128)(2,1)S(1)} %bitcast.20), channel_id=1, replica_groups={{0,8},{16,24},{32,40},{48,56},{64,72},{80,88},{96,104},{112,120},{1,9},..., dimensions={0}, use_global_device_ids=true | all-gather | bytes 589824 | tf_op jit(solution)/shard_map/all_gather | solution.py:375
  93.1 1.0 %place.1 = (f32[64,3072]{1,0:T(8,128)}, f32[1,2,64,64]{3,2,1,0:T(8,128)}, f32[2,64,64]{2,1,0:T(8,128)}) custom-call(bf16[512,384]{1,0:T(8,128)(2,1)S(1)} %all_gather.7.part_ref, f32[1,2,64,64]{3,2,1,0:T(8,128)S(1)} %get-tuple-element.18.prediction_ref, f32[2,64,64]{2,1,0:T(8,128)S(1)} %get-tuple-element.19.grad_ref), custom_call_target="tpu_custom_call" | custom-call | tf_op jit(solution)/shard_map/place/pallas_call | solution.py:377
  (1 shorter events, 0.0 us)
Async XLA Ops:
  0.6 27.4 %copy-start.1 = (f32[2,64,64]{2,1,0:T(8,128)S(1)}, f32[2,64,64]{2,1,0:T(8,128)}, u32[]{:S(2)}) copy-start(f32[2,64,64]{2,1,0:T(8,128)} %prev_ref.3) | copy-start | bytes 98308
  0.6 27.4 %copy-start.2 = (bf16[2,64,64]{2,1,0:T(8,128)(2,1)S(1)}, bf16[2,64,64]{2,1,0:T(8,128)(2,1)}, u32[]{:S(2)}) copy-start(bf16[2,64,64]{2,1,0:T(8,128)(2,1)} %noise_ref.3) | copy-start | bytes 49156
  0.7 27.4 %copy-start.3 = (bf16[2,64,64]{2,1,0:T(8,128)(2,1)S(1)}, bf16[2,64,64]{2,1,0:T(8,128)(2,1)}, u32[]{:S(2)}) copy-start(bf16[2,64,64]{2,1,0:T(8,128)(2,1)} %gen_ref.1) | copy-start | bytes 49156
  0.7 45.0 %copy-start = (bf16[2,64,3072]{2,1,0:T(8,128)(2,1)S(1)}, bf16[2,64,3072]{2,1,0:T(8,128)(2,1)}, u32[]{:S(2)}) copy-start(bf16[2,64,3072]{2,1,0:T(8,128)(2,1)} %saved_ref.1) | copy-start | bytes 2359300

commit v7 on v6

--- a/solution.py
+++ b/solution.py
@@ -179,7 +179,7 @@
     return 2.5 * moved_ref[1].astype(F32) - 1.5 * moved_ref[2].astype(F32)
 
 
-def partial_kernel(moved_ref, noise_ref, prev_ref, local_ref, saved_ref, out_ref):
+def partial_kernel(moved_ref, noise_ref, prev_ref, local_ref, saved_ref, keep_ref, give_ref):
     level = level_rows(local_ref, 64)[1]
     guided = guidance(moved_ref)
     down = moved_ref[3].astype(F32) - guided
@@ -191,8 +191,6 @@
         gap = jnp.abs(prev_ref[i] - real)
         sums.append(jnp.sum(jnp.sum(gap, axis=0, keepdims=True), axis=1, keepdims=True))
     sums = jnp.where(row < 8, sums[0], sums[1])
-    high = sums.astype(BF16).astype(F32)
-    sums = jnp.where(left_half((16, 128)), high, sums - high).astype(BF16)
     tokens = jnp.concatenate([down[:, halves[0]], down[:, halves[1]]], axis=0).astype(BF16)
     out_row = lax.broadcasted_iota(jnp.int32, (128, 64), 0)
     channel = lax.broadcasted_iota(jnp.int32, (128, 64), 1)
@@ -201,19 +199,33 @@
     image = (lax.broadcasted_iota(jnp.int32, (128, 128), 0) % 16) // 8
     owner = lax.broadcasted_iota(jnp.int32, (128, 128), 1) // 64
     spread_out = jnp.where(image == owner, spread_out, 0.0).astype(BF16)
-    lanes = pl.ds(pl.multiple_of(lax.axis_index("group") * 768, 128), 768)
-    saved = jnp.concatenate([saved_ref[0, :, lanes], saved_ref[1, :, lanes]], axis=0)
-    grad = dot(spread_out, saved).astype(BF16)
-    for a in range(8):
-        for b in range(2):
-            out_ref[2 * a + b, :, 0:384] = grad[16 * a : 16 * a + 16, 384 * b : 384 * b + 384]
-            out_ref[2 * a + b, :, 384:512] = sums
+    core = lax.rem(lax.axis_index("seq"), 2)
+    for half, ref in ((1 - core, give_ref), (core, keep_ref)):
+        first = lax.axis_index("group") * 768 + half * 384
+        lanes = pl.ds(pl.multiple_of(first, 128), 384)
+        saved = jnp.concatenate([saved_ref[0, :, lanes], saved_ref[1, :, lanes]], axis=0)
+        ref[:, 0:384] = dot(spread_out, saved).astype(ref.dtype)
+    keep_ref[0:16, 384:512] = sums
+    give_ref[:, 384:512] = jnp.concatenate([split_sums(sums)] * 8, axis=0)
+
+
+def split_sums(sums):
+    high = sums.astype(BF16).astype(F32)
+    return jnp.where(left_half((16, 128)), high, sums - high).astype(BF16)
+
+
+def merge_kernel(keep_ref, given_ref, out_ref):
+    out_ref[:, 0:384] = (keep_ref[:, 0:384] + given_ref[:, 0:384].astype(F32)).astype(BF16)
+    given = given_ref[0:16, 384:448].astype(F32) + given_ref[0:16, 448:512].astype(F32)
+    sums = split_sums(keep_ref[0:16, 384:512] + jnp.concatenate([given, given], axis=1))
+    for at in range(0, out_ref.shape[0], 16):
+        out_ref[at : at + 16, 384:512] = sums
 
 
 def scale_kernel(factor, part_ref, moved_ref, out_ref, grad_ref):
-    total = part_ref[0].astype(F32)
-    for s in range(1, part_ref.shape[0]):
-        total = total + part_ref[s].astype(F32)
+    total = part_ref[0:16, :].astype(F32)
+    for at in range(16, part_ref.shape[0], 16):
+        total = total + part_ref[at : at + 16, :].astype(F32)
     spread = (total[:, 384:385] + total[:, 448:449]) * (1.0 / (NTOK * 64)) + 1e-05
     grad = total[:, 0:384] * (factor / spread)
     grad = grad[0:8] + grad[8:16]
@@ -335,15 +347,26 @@
     )
     moved = lax.all_to_all(moved, "group", 0, 0, tiled=True)
 
-    parts = pl.pallas_call(
+    chips = heads // 2
+    keep, give = pl.pallas_call(
         partial_kernel,
-        out_shape=shape_of((heads, 16, 512), BF16),
+        out_shape=(pltpu.VMEM((16 * chips, 512), F32), shape_of((16 * chips, 512), BF16)),
         in_specs=[VECTOR] * 5,
-        out_specs=VECTOR,
+        out_specs=(VECTOR, VECTOR),
         compiler_params=params(16),
         name="partial",
     )(moved, noise_score, prev_latents, local, saved_features)
-    parts = lax.all_to_all(parts, "seq", 0, 0, tiled=True)
+    given = lax.ppermute(give, "seq", [(k, k ^ 1) for k in range(heads)])
+    parts = pl.pallas_call(
+        merge_kernel,
+        out_shape=shape_of((16 * chips, 512), BF16),
+        in_specs=[VECTOR] * 2,
+        out_specs=VECTOR,
+        compiler_params=params(16),
+        name="merge",
+    )(keep, given)
+    same_part = [[2 * y + core for y in range(chips)] for core in range(2)]
+    parts = lax.all_to_all(parts, "seq", 0, 0, tiled=True, axis_index_groups=same_part)
 
     factor = 1.0 / math.sqrt(2 * copies * NTOK)
     summed, dmd_grad = pl.pallas_call(
@@ -356,7 +379,6 @@
     )(parts, moved)
     summed = lax.all_to_all(summed, "dp", 0, 0, tiled=True)
 
-    chips = heads // 2
     rows = pl.pallas_call(
         sum_kernel,
         out_shape=shape_of((groups * chips * 8, 384), BF16),

time: 94.3 us -> 95 us (level)
  blocking collectives: 84.9 us -> 80.8 us
  starting transfers between devices: 0 us -> 3.64 us
  waiting for transfers between devices: 0 us -> 0.96 us
    all_to_all x1, blocking collectives: 17.6 us -> 11.7 us  [per_device(): lax.all_to_all(parts, 'seq', 0, 0, tiled=True, axis_index_groups=same_part)]
    ppermute x0 -> x1, starting transfers between devices: none -> 3.64 us  [per_device(): given = lax.ppermute(give, 'seq', [(k, k ^ 1) for k in range(heads)])]
    all_gather x1, blocking collectives: 4.69 us -> 6.26 us  [per_device(): lax.all_gather(rows, 'seq', axis=0, tiled=True, axis_index_groups=one_chip)]
    ppermute x0 -> x1, waiting for transfers between devices: none -> 0.96 us  [per_device(): given = lax.ppermute(give, 'seq', [(k, k ^ 1) for k in range(heads)])]
  transfers between devices with their start and end apart: 0 -> 1, of which waited for: 0 -> 1; matrix products, arithmetic and copies ran while one was open for 0% -> 0% of each run, Pallas kernels for 0% -> 0%
where the time goes in v7:
time: 95 us; the launch traced here: 94.7 us
  blocking collectives  80.8 us (85%)
  Pallas kernels  8.55 us (9%)
  starting transfers between devices  3.64 us (4%)
  waiting for transfers between devices  0.96 us (1%)
    all_gather x1, blocking collectives, per_device(): lax.all_gather(sent, 'seq', axis=0, tiled=True).reshape(heads, ROWS, 128)  23.8 us
    all_to_all x1, blocking collectives, per_device(): lax.all_to_all(rows, ('group', 'seq'), 0, 0, tiled=True, axis_index_group...  15 us
    all_to_all x1, blocking collectives, per_device(): moved = lax.all_to_all(moved, 'group', 0, 0, tiled=True)  14.4 us
    all_to_all x1, blocking collectives, per_device(): lax.all_to_all(parts, 'seq', 0, 0, tiled=True, axis_index_groups=same_part)  11.7 us
    all_to_all x1, blocking collectives, per_device(): summed = lax.all_to_all(summed, 'dp', 0, 0, tiled=True)  9.65 us
    all_gather x1, blocking collectives, per_device(): lax.all_gather(rows, 'seq', axis=0, tiled=True, axis_index_groups=one_chip)  6.26 us
    ppermute x1, starting transfers between devices, per_device(): given = lax.ppermute(give, 'seq', [(k, k ^ 1) for k in range(heads)])  3.64 us
    pallas_call x1, Pallas kernels, fold(): pl.pallas_call(fold_kernel, out_shape=(pltpu.VMEM((ROWS, 128), BF16), plt...  3.56 us
  transfers between devices with their start and end apart: 1, of which 1 were waited for; matrix products, arithmetic and copies ran while one was open for 0% of the time, Pallas kernels for 0%

profile of v7, /device:TPU:1, one launch (start us, length us, event | category | flops | bytes accessed | tf_op | source)
XLA Modules:
  0.0 94.7 jit_solution(7235638261372882024)
XLA Ops:
  0.6 0.0 copy-start.1
  0.6 0.0 copy-start.2
  0.7 0.0 copy-start.3
  0.7 0.0 copy-start
  0.7 3.6 %fold.1 = (bf16[208,128]{1,0:T(8,128)(2,1)S(1)}, bf16[64,128]{1,0:T(8,128)(2,1)S(1)}, f32[144,128]{1,0:T(8,128)S(1)}) custom-call(f32[2,64,64]{2,1,0:T(8,128)} %prev_ref.3, bf16[2,64,64]{2,1,0:T(8,128)(2,1)} %gen_ref.1, bf16[2,64,64]{2,1,0:T(8,128)(2,1)} %noise_ref.3, bf16[1,64,3072]{2,1,0:T(8,128)(2,1)} %refs_3_.1, f32[1,3072]{1,0:T(1,128)} %refs_4_.1, ...), custom_call_target="tpu_custom_call" | custom-call | tf_op jit(solution)/shard_map/fold/pallas_call | solution.py:286
  4.2 23.8 %all_gather.6 = bf16[3328,128]{1,0:T(8,128)(2,1)S(1)} all-gather(bf16[208,128]{1,0:T(8,128)(2,1)S(1)} %get-tuple-element.15), channel_id=1, replica_groups=mesh['group'=4,'seq'=16,'dp'=8] {'seq'}, dimensions={0}, use_global_device_ids=true | all-gather | bytes 905216 | tf_op jit(solution)/shard_map/all_gather | solution.py:343
  28.0 0.0 copy-done.1
  28.0 0.0 copy-done.2
  28.0 0.0 copy-done.3
  28.0 3.2 %attend.1 = (bf16[4,64,128]{2,1,0:T(8,128)(2,1)S(1)}, f32[1,2,64,64]{3,2,1,0:T(8,128)S(1)}) custom-call(bf16[2,64,64]{2,1,0:T(8,128)(2,1)S(1)} %copy-done.3, bf16[2,64,64]{2,1,0:T(8,128)(2,1)S(1)} %copy-done.2, f32[2,64,64]{2,1,0:T(8,128)S(1)} %copy-done.1, bf16[16,208,128]{2,1,0:T(8,128)(2,1)S(1)} %bitcast.17, ...), custom_call_target="tpu_custom_call" | custom-call | tf_op jit(solution)/shard_map/attend/pallas_call | solution.py:306
  31.2 14.4 %all_to_all.39.moved_ref.refs_1_ = bf16[4,64,128]{2,1,0:T(8,128)(2,1)S(1)} all-to-all(bf16[4,64,128]{2,1,0:T(8,128)(2,1)S(1)} %get-tuple-element.18), channel_id=1, replica_groups=mesh['group'=4,'seq'=16,'dp'=8] {'group'}, dimensions={0} | all-to-all | bytes 131072 | tf_op jit(solution)/shard_map/all_to_all | solution.py:348
  45.6 0.0 copy-done
  45.6 0.5 partial.1
  46.1 3.6 %collective-permute-start = (bf16[128,512]{1,0:T(8,128)(2,1)S(1)}, bf16[128,512]{1,0:T(8,128)(2,1)S(1)}, u32[]{:S(2)}, u32[]{:S(2)}) collective-permute-start(bf16[128,512]{1,0:T(8,128)(2,1)S(1)} %get-tuple-element.20), channel_id=1, source_target_pairs={{0,8},{8,0},{16,24},{24,16},{32,40},{40,32},{48,56},{56,48},{64,72... | collective-permute-start | bytes 393224 | tf_op jit(solution)/shard_map/ppermute | solution.py:359
  49.8 1.0 %collective-permute-done.given_ref = bf16[128,512]{1,0:T(8,128)(2,1)S(1)} collective-permute-done((bf16[128,512]{1,0:T(8,128)(2,1)S(1)}, bf16[128,512]{1,0:T(8,128)(2,1)S(1)}, u32[]{:S(2)}, u32[]{:S(2)}) %collective-permute-start) | collective-permute-done | bytes 131104 | tf_op jit(solution)/shard_map/ppermute | solution.py:359
  50.7 0.1 merge.1
  50.9 11.7 %all_to_all.40 = bf16[8,16,512]{2,1,0:T(8,128)(2,1)S(1)} all-to-all(bf16[8,16,512]{2,1,0:T(8,128)(2,1)S(1)} %bitcast.20), channel_id=1, replica_groups={{0,16,32,48,64,80,96,112},{8,24,40,56,72,88,104,120},{1,17,33,49,65,81,..., dimensions={0} | all-to-all | bytes 262144 | tf_op jit(solution)/shard_map/all_to_all | solution.py:369
  62.6 0.2 scale.1
  62.8 9.7 %all_to_all.41 = bf16[8,8,384]{2,1,0:T(8,128)(2,1)S(1)} all-to-all(bf16[8,8,384]{2,1,0:T(8,128)(2,1)S(1)} %bitcast.22), channel_id=1, replica_groups=mesh['group'=4,'seq'=16,'dp'=8] {'dp'}, dimensions={0} | all-to-all | bytes 98304 | tf_op jit(solution)/shard_map/all_to_all | solution.py:380
  72.5 15.0 %all_to_all.42 = bf16[32,8,384]{2,1,0:T(8,128)(2,1)S(1)} all-to-all(bf16[32,8,384]{2,1,0:T(8,128)(2,1)S(1)} %bitcast.18), channel_id=1, replica_groups={{0,16,32,48,64,80,96,112,128,144,160,176,192,208,224,240,256,272,288,30..., dimensions={0} | all-to-all | bytes 393216 | tf_op jit(solution)/shard_map/all_to_all | solution.py:393
  87.5 6.3 %all_gather.7.part_ref = bf16[512,384]{1,0:T(8,128)(2,1)S(1)} all-gather(bf16[256,384]{1,0:T(8,128)(2,1)S(1)} %bitcast.24), channel_id=1, replica_groups={{0,8},{16,24},{32,40},{48,56},{64,72},{80,88},{96,104},{112,120},{1,9},..., dimensions={0}, use_global_device_ids=true | all-gather | bytes 589824 | tf_op jit(solution)/shard_map/all_gather | solution.py:397
  93.7 1.0 %place.1 = (f32[64,3072]{1,0:T(8,128)}, f32[1,2,64,64]{3,2,1,0:T(8,128)}, f32[2,64,64]{2,1,0:T(8,128)}) custom-call(bf16[512,384]{1,0:T(8,128)(2,1)S(1)} %all_gather.7.part_ref, f32[1,2,64,64]{3,2,1,0:T(8,128)S(1)} %get-tuple-element.22.prediction_ref, f32[2,64,64]{2,1,0:T(8,128)S(1)} %get-tuple-element.23.grad_ref), custom_call_target="tpu_custom_call" | custom-call | tf_op jit(solution)/shard_map/place/pallas_call | solution.py:399
  (1 shorter events, 0.0 us)
Async XLA Ops:
  0.6 27.4 %copy-start.1 = (f32[2,64,64]{2,1,0:T(8,128)S(1)}, f32[2,64,64]{2,1,0:T(8,128)}, u32[]{:S(2)}) copy-start(f32[2,64,64]{2,1,0:T(8,128)} %prev_ref.3) | copy-start | bytes 98308
  0.6 27.4 %copy-start.2 = (bf16[2,64,64]{2,1,0:T(8,128)(2,1)S(1)}, bf16[2,64,64]{2,1,0:T(8,128)(2,1)}, u32[]{:S(2)}) copy-start(bf16[2,64,64]{2,1,0:T(8,128)(2,1)} %noise_ref.3) | copy-start | bytes 49156
  0.7 27.4 %copy-start.3 = (bf16[2,64,64]{2,1,0:T(8,128)(2,1)S(1)}, bf16[2,64,64]{2,1,0:T(8,128)(2,1)}, u32[]{:S(2)}) copy-start(bf16[2,64,64]{2,1,0:T(8,128)(2,1)} %gen_ref.1) | copy-start | bytes 49156
  0.7 45.0 %copy-start = (bf16[2,64,3072]{2,1,0:T(8,128)(2,1)S(1)}, bf16[2,64,3072]{2,1,0:T(8,128)(2,1)}, u32[]{:S(2)}) copy-start(bf16[2,64,3072]{2,1,0:T(8,128)(2,1)} %saved_ref.1) | copy-start | bytes 2359300
  46.1 4.6 %collective-permute-start = (bf16[128,512]{1,0:T(8,128)(2,1)S(1)}, bf16[128,512]{1,0:T(8,128)(2,1)S(1)}, u32[]{:S(2)}, u32[]{:S(2)}) collective-permute-start(bf16[128,512]{1,0:T(8,128)(2,1)S(1)} %get-tuple-element.20), channel_id=1, source_target_pairs={{0,8},{8,0},{16,24},{24,16},{32,40},{40,32},{48,56},{56,48},{64,72... | collective-permute-start | bytes 393224 | tf_op jit(solution)/shard_map/ppermute | solution.py:359

commit v8 on v6

--- a/solution.py
+++ b/solution.py
@@ -91,38 +91,29 @@
     own = jnp.concatenate([scaled[0:64], scaled[64:128]], axis=1)
     sent_ref[144:208, :] = own
     own_ref[...] = own
-    const = [part[128:129] + part[129:130] for part in folded]
-    final_const = final[128:129] + final[129:130]
-    factor = math.log2(math.e) / math.sqrt(128.0)
+    q, k, v, f = [
+        [part[0:64] + value * part[64:128] for value in used]
+        for part in (*folded, jnp.concatenate([final, final], axis=1))
+    ]
+    q.append(jnp.broadcast_to(folded[0][128:129] + folded[0][129:130], (16, 128)))
+    v.append(jnp.broadcast_to(folded[2][128:129] + folded[2][129:130], (16, 128)))
+    q, k, v = [jnp.concatenate(part, axis=0).astype(BF16) for part in (q, k, v)]
     w_out = w_out_ref[...]
-    blocks, consts, locals_ = [], [], []
-    value_const = dot(jnp.broadcast_to(const[2], (16, 128)).astype(BF16), w_out, 1, 1)
-    for i in range(2):
-        q, k, v = [(part[0:64] + used[i] * part[64:128]) for part in folded]
-        kb = k.astype(BF16)
-        scores = dot(q.astype(BF16), kb, 1, 1) * factor
-        out = dot(v.astype(BF16), w_out, 1, 1)
-        key_const = dot(jnp.broadcast_to(const[0], (16, 128)).astype(BF16), kb, 1, 1) * factor
-        local = final[0:64] + used[i] * final[64:128]
-        zero = jnp.zeros_like(local)
-        if i == 0:
-            blocks.append(jnp.concatenate([scores, out], axis=1))
-            consts.append(jnp.concatenate([key_const, value_const], axis=1))
-            locals_.append(jnp.concatenate([zero, local], axis=1))
-        else:
-            blocks.append(jnp.concatenate([out, scores], axis=1))
-            consts.append(jnp.concatenate([value_const, key_const], axis=1))
-            locals_.append(jnp.concatenate([local, zero], axis=1))
-    sent_ref[0:64, :] = blocks[0].astype(BF16)
-    sent_ref[64:128, :] = blocks[1].astype(BF16)
-    row = lax.broadcasted_iota(jnp.int32, (16, 128), 0)
-    sent_ref[128:144, :] = jnp.where(row == 0, consts[0], consts[1]).astype(BF16)
-    local_ref[0:64, :] = locals_[0]
-    local_ref[64:128, :] = locals_[1]
-    both = jnp.concatenate([final_const, final_const], axis=1)
+    scores = dot(q, k, 1, 1) * (math.log2(math.e) / math.sqrt(128.0))
+    out = dot(v, jnp.concatenate([w_out, w_out], axis=0), 1, 1)
+    left = left_half((64, 128))
+    sent_ref[0:64, :] = jnp.where(left, scores[0:64], out[0:64]).astype(BF16)
+    sent_ref[64:128, :] = jnp.where(left, out[64:128], scores[64:128]).astype(BF16)
+    odd = lax.broadcasted_iota(jnp.int32, (16, 128), 0) > 0
+    own_side = jnp.logical_xor(left_half((16, 128)), odd)
+    sent_ref[128:144, :] = jnp.where(own_side, scores[128:144], out[128:144]).astype(BF16)
+    local_ref[0:64, :] = f[0]
+    local_ref[64:128, :] = f[1]
+    both = final[128:129] + final[129:130]
+    both = jnp.concatenate([both, both], axis=1)
     local_ref[128:136, :] = jnp.broadcast_to(both, (8, 128))
-    for k, value in enumerate([gen, *level, *used]):
-        local_ref[136 + k : 137 + k, :] = jnp.full((1, 128), value, F32)
+    for n, value in enumerate([gen, *level, *used]):
+        local_ref[136 + n : 137 + n, :] = jnp.full((1, 128), value, F32)
 
 
 def attend_kernel(

time: 94.3 us -> 94.2 us (level)
  no operation moved by 1% of the time
where the time goes in v8:
time: 94.2 us; the launch traced here: 94 us
  blocking collectives  85 us (90%)
  Pallas kernels  8.31 us (9%)
    all_gather x1, blocking collectives, per_device(): lax.all_gather(sent, 'seq', axis=0, tiled=True).reshape(heads, ROWS, 128)  23.8 us
    all_to_all x1, blocking collectives, per_device(): parts = lax.all_to_all(parts, 'seq', 0, 0, tiled=True)  17.6 us
    all_to_all x1, blocking collectives, per_device(): lax.all_to_all(rows, ('group', 'seq'), 0, 0, tiled=True, axis_index_group...  14.8 us
    all_to_all x1, blocking collectives, per_device(): moved = lax.all_to_all(moved, 'group', 0, 0, tiled=True)  14.4 us
    all_to_all x1, blocking collectives, per_device(): summed = lax.all_to_all(summed, 'dp', 0, 0, tiled=True)  9.64 us
    all_gather x1, blocking collectives, per_device(): lax.all_gather(rows, 'seq', axis=0, tiled=True, axis_index_groups=one_chip)  4.71 us
    pallas_call x1, Pallas kernels, fold(): pl.pallas_call(fold_kernel, out_shape=(pltpu.VMEM((ROWS, 128), BF16), plt...  3.46 us
    pallas_call x1, Pallas kernels, attend(): pl.pallas_call(attend_kernel, out_shape=(shape_of((groups, 64, 128), BF16...  3.16 us

profile of v8, /device:TPU:1, one launch (start us, length us, event | category | flops | bytes accessed | tf_op | source)
XLA Modules:
  0.0 94.0 jit_solution(7984388860675319969)
XLA Ops:
  0.6 0.0 copy-start.1
  0.6 0.0 copy-start.2
  0.7 0.0 copy-start.3
  0.7 0.0 copy-start
  0.7 3.5 %fold.1 = (bf16[208,128]{1,0:T(8,128)(2,1)S(1)}, bf16[64,128]{1,0:T(8,128)(2,1)S(1)}, f32[144,128]{1,0:T(8,128)S(1)}) custom-call(f32[2,64,64]{2,1,0:T(8,128)} %prev_ref.3, bf16[2,64,64]{2,1,0:T(8,128)(2,1)} %gen_ref.1, bf16[2,64,64]{2,1,0:T(8,128)(2,1)} %noise_ref.3, bf16[1,64,3072]{2,1,0:T(8,128)(2,1)} %refs_3_.1, f32[1,3072]{1,0:T(1,128)} %refs_4_.1, ...), custom_call_target="tpu_custom_call" | custom-call | tf_op jit(solution)/shard_map/fold/pallas_call | solution.py:265
  4.1 23.8 %all_gather.6 = bf16[3328,128]{1,0:T(8,128)(2,1)S(1)} all-gather(bf16[208,128]{1,0:T(8,128)(2,1)S(1)} %get-tuple-element.13), channel_id=1, replica_groups=mesh['group'=4,'seq'=16,'dp'=8] {'seq'}, dimensions={0}, use_global_device_ids=true | all-gather | bytes 905216 | tf_op jit(solution)/shard_map/all_gather | solution.py:322
  27.9 0.0 copy-done.1
  27.9 0.0 copy-done.2
  27.9 0.0 copy-done.3
  27.9 3.2 %attend.1 = (bf16[4,64,128]{2,1,0:T(8,128)(2,1)S(1)}, f32[1,2,64,64]{3,2,1,0:T(8,128)S(1)}) custom-call(bf16[2,64,64]{2,1,0:T(8,128)(2,1)S(1)} %copy-done.3, bf16[2,64,64]{2,1,0:T(8,128)(2,1)S(1)} %copy-done.2, f32[2,64,64]{2,1,0:T(8,128)S(1)} %copy-done.1, bf16[16,208,128]{2,1,0:T(8,128)(2,1)S(1)} %bitcast.15, ...), custom_call_target="tpu_custom_call" | custom-call | tf_op jit(solution)/shard_map/attend/pallas_call | solution.py:285
  31.1 14.4 %all_to_all.33.moved_ref.refs_1_ = bf16[4,64,128]{2,1,0:T(8,128)(2,1)S(1)} all-to-all(bf16[4,64,128]{2,1,0:T(8,128)(2,1)S(1)} %get-tuple-element.16), channel_id=1, replica_groups=mesh['group'=4,'seq'=16,'dp'=8] {'group'}, dimensions={0} | all-to-all | bytes 131072 | tf_op jit(solution)/shard_map/all_to_all | solution.py:327
  45.5 0.0 copy-done
  45.5 0.5 partial.1
  46.0 17.6 %all_to_all.34.refs_0_ = bf16[16,16,512]{2,1,0:T(8,128)(2,1)S(1)} all-to-all(bf16[16,16,512]{2,1,0:T(8,128)(2,1)S(1)} %partial.1), channel_id=1, replica_groups=mesh['group'=4,'seq'=16,'dp'=8] {'seq'}, dimensions={0} | all-to-all | bytes 524288 | tf_op jit(solution)/shard_map/all_to_all | solution.py:337
  63.6 0.2 scale.1
  63.8 9.6 %all_to_all.35 = bf16[8,8,384]{2,1,0:T(8,128)(2,1)S(1)} all-to-all(bf16[8,8,384]{2,1,0:T(8,128)(2,1)S(1)} %bitcast.18), channel_id=1, replica_groups=mesh['group'=4,'seq'=16,'dp'=8] {'dp'}, dimensions={0} | all-to-all | bytes 98304 | tf_op jit(solution)/shard_map/all_to_all | solution.py:348
  73.4 14.8 %all_to_all.36 = bf16[32,8,384]{2,1,0:T(8,128)(2,1)S(1)} all-to-all(bf16[32,8,384]{2,1,0:T(8,128)(2,1)S(1)} %bitcast.16), channel_id=1, replica_groups={{0,16,32,48,64,80,96,112,128,144,160,176,192,208,224,240,256,272,288,30..., dimensions={0} | all-to-all | bytes 393216 | tf_op jit(solution)/shard_map/all_to_all | solution.py:362
  88.3 4.7 %all_gather.7.part_ref = bf16[512,384]{1,0:T(8,128)(2,1)S(1)} all-gather(bf16[256,384]{1,0:T(8,128)(2,1)S(1)} %bitcast.20), channel_id=1, replica_groups={{0,8},{16,24},{32,40},{48,56},{64,72},{80,88},{96,104},{112,120},{1,9},..., dimensions={0}, use_global_device_ids=true | all-gather | bytes 589824 | tf_op jit(solution)/shard_map/all_gather | solution.py:366
  93.0 1.0 %place.1 = (f32[64,3072]{1,0:T(8,128)}, f32[1,2,64,64]{3,2,1,0:T(8,128)}, f32[2,64,64]{2,1,0:T(8,128)}) custom-call(bf16[512,384]{1,0:T(8,128)(2,1)S(1)} %all_gather.7.part_ref, f32[1,2,64,64]{3,2,1,0:T(8,128)S(1)} %get-tuple-element.18.prediction_ref, f32[2,64,64]{2,1,0:T(8,128)S(1)} %get-tuple-element.19.grad_ref), custom_call_target="tpu_custom_call" | custom-call | tf_op jit(solution)/shard_map/place/pallas_call | solution.py:368
  (1 shorter events, 0.0 us)
Async XLA Ops:
  0.6 27.3 %copy-start.1 = (f32[2,64,64]{2,1,0:T(8,128)S(1)}, f32[2,64,64]{2,1,0:T(8,128)}, u32[]{:S(2)}) copy-start(f32[2,64,64]{2,1,0:T(8,128)} %prev_ref.3) | copy-start | bytes 98308
  0.6 27.3 %copy-start.2 = (bf16[2,64,64]{2,1,0:T(8,128)(2,1)S(1)}, bf16[2,64,64]{2,1,0:T(8,128)(2,1)}, u32[]{:S(2)}) copy-start(bf16[2,64,64]{2,1,0:T(8,128)(2,1)} %noise_ref.3) | copy-start | bytes 49156
  0.7 27.3 %copy-start.3 = (bf16[2,64,64]{2,1,0:T(8,128)(2,1)S(1)}, bf16[2,64,64]{2,1,0:T(8,128)(2,1)}, u32[]{:S(2)}) copy-start(bf16[2,64,64]{2,1,0:T(8,128)(2,1)} %gen_ref.1) | copy-start | bytes 49156
  0.7 44.9 %copy-start = (bf16[2,64,3072]{2,1,0:T(8,128)(2,1)S(1)}, bf16[2,64,3072]{2,1,0:T(8,128)(2,1)}, u32[]{:S(2)}) copy-start(bf16[2,64,3072]{2,1,0:T(8,128)(2,1)} %saved_ref.1) | copy-start | bytes 2359300

commit v9 on v8

--- a/solution.py
+++ b/solution.py
@@ -175,15 +175,15 @@
     guided = guidance(moved_ref)
     down = moved_ref[3].astype(F32) - guided
     halves = (slice(64, 128), slice(0, 64))
-    row = lax.broadcasted_iota(jnp.int32, (16, 128), 0)
+    row = lax.broadcasted_iota(jnp.int32, (8, 128), 0)
     sums = []
     for i in range(2):
         real = noisy_latent(level[i], prev_ref[i], noise_ref[i]) - guided[:, halves[i]]
         gap = jnp.abs(prev_ref[i] - real)
         sums.append(jnp.sum(jnp.sum(gap, axis=0, keepdims=True), axis=1, keepdims=True))
-    sums = jnp.where(row < 8, sums[0], sums[1])
+    sums = jnp.where(row < 4, sums[0], sums[1])
     high = sums.astype(BF16).astype(F32)
-    sums = jnp.where(left_half((16, 128)), high, sums - high).astype(BF16)
+    sums = jnp.where(left_half((8, 128)), high, sums - high).astype(BF16)
     tokens = jnp.concatenate([down[:, halves[0]], down[:, halves[1]]], axis=0).astype(BF16)
     out_row = lax.broadcasted_iota(jnp.int32, (128, 64), 0)
     channel = lax.broadcasted_iota(jnp.int32, (128, 64), 1)
@@ -197,23 +197,26 @@
     grad = dot(spread_out, saved).astype(BF16)
     for a in range(8):
         for b in range(2):
-            out_ref[2 * a + b, :, 0:384] = grad[16 * a : 16 * a + 16, 384 * b : 384 * b + 384]
-            out_ref[2 * a + b, :, 384:512] = sums
+            for k in range(3):
+                lane = 384 * b + 128 * k
+                part = grad[16 * a : 16 * a + 16, lane : lane + 128]
+                out_ref[2 * a + b, 16 * k : 16 * k + 16, :] = part
+            out_ref[2 * a + b, 48:56, :] = sums
 
 
 def scale_kernel(factor, part_ref, moved_ref, out_ref, grad_ref):
     total = part_ref[0].astype(F32)
     for s in range(1, part_ref.shape[0]):
         total = total + part_ref[s].astype(F32)
-    spread = (total[:, 384:385] + total[:, 448:449]) * (1.0 / (NTOK * 64)) + 1e-05
-    grad = total[:, 0:384] * (factor / spread)
-    grad = grad[0:8] + grad[8:16]
+    spread = (total[48:56, 0:1] + total[48:56, 64:65]) * (1.0 / (NTOK * 64)) + 1e-05
+    grad = jnp.concatenate([total[0:16], total[16:32], total[32:48]], axis=1)
+    grad = grad[0:8] * (factor / spread[0:1]) + grad[8:16] * (factor / spread[4:5])
     pair = jnp.concatenate([grad, grad], axis=0).astype(BF16)
     for at in range(0, out_ref.shape[0], 16):
         out_ref[at : at + 16, :] = pair
     gap = guidance(moved_ref) - moved_ref[3].astype(F32)
     grad_ref[0] = gap[:, 64:128] / spread[0:1]
-    grad_ref[1] = gap[:, 0:64] / spread[8:9]
+    grad_ref[1] = gap[:, 0:64] / spread[4:5]
 
 
 def sum_kernel(part_ref, out_ref):
@@ -328,7 +331,7 @@
 
     parts = pl.pallas_call(
         partial_kernel,
-        out_shape=shape_of((heads, 16, 512), BF16),
+        out_shape=shape_of((heads, 56, 128), BF16),
         in_specs=[VECTOR] * 5,
         out_specs=VECTOR,
         compiler_params=params(16),

time: 94.2 us -> 93.5 us (level)
  no operation moved by 1% of the time
where the time goes in v9:
time: 93.5 us; the launch traced here: 93.3 us
  blocking collectives  84.3 us (90%)
  Pallas kernels  8.32 us (9%)
    all_gather x1, blocking collectives, per_device(): lax.all_gather(sent, 'seq', axis=0, tiled=True).reshape(heads, ROWS, 128)  23.8 us
    all_to_all x1, blocking collectives, per_device(): parts = lax.all_to_all(parts, 'seq', 0, 0, tiled=True)  16.9 us
    all_to_all x1, blocking collectives, per_device(): lax.all_to_all(rows, ('group', 'seq'), 0, 0, tiled=True, axis_index_group...  14.8 us
    all_to_all x1, blocking collectives, per_device(): moved = lax.all_to_all(moved, 'group', 0, 0, tiled=True)  14.4 us
    all_to_all x1, blocking collectives, per_device(): summed = lax.all_to_all(summed, 'dp', 0, 0, tiled=True)  9.64 us
    all_gather x1, blocking collectives, per_device(): lax.all_gather(rows, 'seq', axis=0, tiled=True, axis_index_groups=one_chip)  4.68 us
    pallas_call x1, Pallas kernels, fold(): pl.pallas_call(fold_kernel, out_shape=(pltpu.VMEM((ROWS, 128), BF16), plt...  3.46 us
    pallas_call x1, Pallas kernels, attend(): pl.pallas_call(attend_kernel, out_shape=(shape_of((groups, 64, 128), BF16...  3.16 us

profile of v9, /device:TPU:1, one launch (start us, length us, event | category | flops | bytes accessed | tf_op | source)
XLA Modules:
  0.0 93.3 jit_solution(824863577877984738)
XLA Ops:
  0.6 0.0 copy-start.1
  0.6 0.0 copy-start.2
  0.7 0.0 copy-start.3
  0.7 0.0 copy-start
  0.7 3.5 %fold.1 = (bf16[208,128]{1,0:T(8,128)(2,1)S(1)}, bf16[64,128]{1,0:T(8,128)(2,1)S(1)}, f32[144,128]{1,0:T(8,128)S(1)}) custom-call(f32[2,64,64]{2,1,0:T(8,128)} %prev_ref.3, bf16[2,64,64]{2,1,0:T(8,128)(2,1)} %gen_ref.1, bf16[2,64,64]{2,1,0:T(8,128)(2,1)} %noise_ref.3, bf16[1,64,3072]{2,1,0:T(8,128)(2,1)} %refs_3_.1, f32[1,3072]{1,0:T(1,128)} %refs_4_.1, ...), custom_call_target="tpu_custom_call" | custom-call | tf_op jit(solution)/shard_map/fold/pallas_call | solution.py:268
  4.1 23.8 %all_gather.6 = bf16[3328,128]{1,0:T(8,128)(2,1)S(1)} all-gather(bf16[208,128]{1,0:T(8,128)(2,1)S(1)} %get-tuple-element.13), channel_id=1, replica_groups=mesh['group'=4,'seq'=16,'dp'=8] {'seq'}, dimensions={0}, use_global_device_ids=true | all-gather | bytes 905216 | tf_op jit(solution)/shard_map/all_gather | solution.py:325
  27.9 0.0 copy-done.1
  27.9 0.0 copy-done.2
  27.9 0.0 copy-done.3
  27.9 3.2 %attend.1 = (bf16[4,64,128]{2,1,0:T(8,128)(2,1)S(1)}, f32[1,2,64,64]{3,2,1,0:T(8,128)S(1)}) custom-call(bf16[2,64,64]{2,1,0:T(8,128)(2,1)S(1)} %copy-done.3, bf16[2,64,64]{2,1,0:T(8,128)(2,1)S(1)} %copy-done.2, f32[2,64,64]{2,1,0:T(8,128)S(1)} %copy-done.1, bf16[16,208,128]{2,1,0:T(8,128)(2,1)S(1)} %bitcast.15, ...), custom_call_target="tpu_custom_call" | custom-call | tf_op jit(solution)/shard_map/attend/pallas_call | solution.py:288
  31.1 14.4 %all_to_all.33.moved_ref.refs_1_ = bf16[4,64,128]{2,1,0:T(8,128)(2,1)S(1)} all-to-all(bf16[4,64,128]{2,1,0:T(8,128)(2,1)S(1)} %get-tuple-element.16), channel_id=1, replica_groups=mesh['group'=4,'seq'=16,'dp'=8] {'group'}, dimensions={0} | all-to-all | bytes 131072 | tf_op jit(solution)/shard_map/all_to_all | solution.py:330
  45.5 0.0 copy-done
  45.5 0.5 partial.1
  46.0 16.9 %all_to_all.34.refs_0_ = bf16[16,56,128]{2,1,0:T(8,128)(2,1)S(1)} all-to-all(bf16[16,56,128]{2,1,0:T(8,128)(2,1)S(1)} %partial.1), channel_id=1, replica_groups=mesh['group'=4,'seq'=16,'dp'=8] {'seq'}, dimensions={0} | all-to-all | bytes 458752 | tf_op jit(solution)/shard_map/all_to_all | solution.py:340
  62.9 0.2 scale.1
  63.1 9.6 %all_to_all.35 = bf16[8,8,384]{2,1,0:T(8,128)(2,1)S(1)} all-to-all(bf16[8,8,384]{2,1,0:T(8,128)(2,1)S(1)} %bitcast.18), channel_id=1, replica_groups=mesh['group'=4,'seq'=16,'dp'=8] {'dp'}, dimensions={0} | all-to-all | bytes 98304 | tf_op jit(solution)/shard_map/all_to_all | solution.py:351
  72.8 14.8 %all_to_all.36 = bf16[32,8,384]{2,1,0:T(8,128)(2,1)S(1)} all-to-all(bf16[32,8,384]{2,1,0:T(8,128)(2,1)S(1)} %bitcast.16), channel_id=1, replica_groups={{0,16,32,48,64,80,96,112,128,144,160,176,192,208,224,240,256,272,288,30..., dimensions={0} | all-to-all | bytes 393216 | tf_op jit(solution)/shard_map/all_to_all | solution.py:365
  87.6 4.7 %all_gather.7.part_ref = bf16[512,384]{1,0:T(8,128)(2,1)S(1)} all-gather(bf16[256,384]{1,0:T(8,128)(2,1)S(1)} %bitcast.20), channel_id=1, replica_groups={{0,8},{16,24},{32,40},{48,56},{64,72},{80,88},{96,104},{112,120},{1,9},..., dimensions={0}, use_global_device_ids=true | all-gather | bytes 589824 | tf_op jit(solution)/shard_map/all_gather | solution.py:369
  92.3 1.0 %place.1 = (f32[64,3072]{1,0:T(8,128)}, f32[1,2,64,64]{3,2,1,0:T(8,128)}, f32[2,64,64]{2,1,0:T(8,128)}) custom-call(bf16[512,384]{1,0:T(8,128)(2,1)S(1)} %all_gather.7.part_ref, f32[1,2,64,64]{3,2,1,0:T(8,128)S(1)} %get-tuple-element.18.prediction_ref, f32[2,64,64]{2,1,0:T(8,128)S(1)} %get-tuple-element.19.grad_ref), custom_call_target="tpu_custom_call" | custom-call | tf_op jit(solution)/shard_map/place/pallas_call | solution.py:371
  (1 shorter events, 0.0 us)
Async XLA Ops:
  0.6 27.3 %copy-start.1 = (f32[2,64,64]{2,1,0:T(8,128)S(1)}, f32[2,64,64]{2,1,0:T(8,128)}, u32[]{:S(2)}) copy-start(f32[2,64,64]{2,1,0:T(8,128)} %prev_ref.3) | copy-start | bytes 98308
  0.6 27.3 %copy-start.2 = (bf16[2,64,64]{2,1,0:T(8,128)(2,1)S(1)}, bf16[2,64,64]{2,1,0:T(8,128)(2,1)}, u32[]{:S(2)}) copy-start(bf16[2,64,64]{2,1,0:T(8,128)(2,1)} %noise_ref.3) | copy-start | bytes 49156
  0.7 27.3 %copy-start.3 = (bf16[2,64,64]{2,1,0:T(8,128)(2,1)S(1)}, bf16[2,64,64]{2,1,0:T(8,128)(2,1)}, u32[]{:S(2)}) copy-start(bf16[2,64,64]{2,1,0:T(8,128)(2,1)} %gen_ref.1) | copy-start | bytes 49156
  0.7 44.9 %copy-start = (bf16[2,64,3072]{2,1,0:T(8,128)(2,1)S(1)}, bf16[2,64,3072]{2,1,0:T(8,128)(2,1)}, u32[]{:S(2)}) copy-start(bf16[2,64,3072]{2,1,0:T(8,128)(2,1)} %saved_ref.1) | copy-start | bytes 2359300
